TPU v7x, 256 devices: a whole 4x4x8 slice. The times are simulated.
256 devices in a mesh: dp: 8 (over y, x_hi), seq: 32 (over x_lo, z, core).
Axes of the slice: x: 4 (x_hi: 2, x_lo: 2; x = x_hi * 2 + x_lo), y: 4, z: 8, core: 2. Of those that a mesh axis runs over, the one named last changes fastest.
Arguments:
- tiles: bfloat16 [8, 16384, 768], P('dp', 'seq'), may hold values from -6 to 6
- cotangent: bfloat16 [8, 16384, 768], P('dp', 'seq'), may hold values from -192 to 192
- gain: bfloat16 [768], replicated, may hold values from 0.5 to 1.5
- query_matrix: bfloat16 [768, 768], replicated, may hold values from -0.21875 to 0.21875
- key_matrix: bfloat16 [768, 768], replicated, may hold values from -0.21875 to 0.21875
- value_matrix: bfloat16 [768, 768], replicated, may hold values from -0.21875 to 0.21875
- w_out: bfloat16 [768, 768], replicated, may hold values from -0.21875 to 0.21875
- query_down_factor: bfloat16 [768, 8], replicated, may hold values from -0.21875 to 0.21875
- query_up_factor: bfloat16 [8, 768], replicated, may hold values from -1.1953125 to 1.1953125
- value_down_factor: bfloat16 [768, 8], replicated, may hold values from -0.21875 to 0.21875
- value_up_factor: bfloat16 [8, 768], replicated, may hold values from -1.1953125 to 1.1953125
- valid_count: int32 [8], P('dp'), may hold values from 8192 to 16384, as said below
Outputs:
- incoming_derivative: bfloat16 [8, 16384, 768], P('dp', 'seq')
- adapter_grads: float32 [4, 8, 768], replicated
Inputs may be any that keep to these rules, and one draw needn't show every extreme that they name: `valid_count`: each slide has at least half of its tiles valid, and in every draw some slide is entirely valid.
All inputs are finite; a program needn't handle non-finite values.
Results may differ from a plain program's by a relative error of at most 0.02.
Values may be sent and summed in bfloat16 or wider, within the bound.
A program may use at most 128 MiB of HBM per device.

v0:
```python
import math

import jax
import jax.numpy as jnp
from jax import lax
from jax.sharding import PartitionSpec as P

HEAD_COUNT = 16
FINE_SEGMENT0 = 512
MIDDLE_DILATION = 4
G_DEV = 16


adapter_scale = 2.0
eps = 1e-05


def partner(shard, axis, apart):
    return lax.ppermute(shard, axis, [(i, i ^ 1 << apart) for i in range(lax.axis_size(axis))])


def layer_normalize(tiles):
    payload_vectors = tiles.astype(jnp.float32)
    center = payload_vectors - jnp.mean(payload_vectors, -1, keepdims=True)
    inverse_deviation = lax.rsqrt(jnp.mean(center * center, -1, keepdims=True) + eps)
    return (center * inverse_deviation, inverse_deviation)


def allowed_keys(query_pos, key_pos, valid):
    return (key_pos[..., None, :] < valid) | (key_pos[..., None, :] == query_pos[..., :, None])


def exponentials(probe_embeddings, address_embeddings, allowed):
    softmax_sharpness = 1.0 / math.sqrt(probe_embeddings.shape[-1])
    similarity_grid = (
        jnp.einsum(
            "...fou,...iou->...ofi",
            probe_embeddings,
            address_embeddings,
            preferred_element_type=jnp.float32,
        )
        * softmax_sharpness
    )
    return jnp.where(allowed[..., None, :, :], jnp.exp(similarity_grid), 0.0)


def weights_of(expo, total_sum):
    return (expo / total_sum[..., None]).astype(jnp.bfloat16)


def value_mixing(probabilities, payload_vectors):
    return jnp.einsum(
        "...fcz,...zfx->...cfx", probabilities, payload_vectors, preferred_element_type=jnp.float32
    )


def score_grads(expo, total_sum, row_delta, result_cotangent, payload_vectors):
    weighting_cotangent = jnp.einsum(
        "...fou,...iou->...ofi",
        result_cotangent,
        payload_vectors,
        preferred_element_type=jnp.float32,
    )
    return (expo / total_sum[..., None] * (weighting_cotangent - row_delta[..., None])).astype(
        jnp.bfloat16
    )


def query_gradients(derivative_sequence, address_embeddings):
    softmax_sharpness = 1.0 / math.sqrt(address_embeddings.shape[-1])
    return (
        jnp.einsum(
            "...fcz,...zfx->...cfx",
            derivative_sequence,
            address_embeddings,
            preferred_element_type=jnp.float32,
        )
        * softmax_sharpness
    )


def key_grads(derivative_sequence, probe_embeddings):
    softmax_sharpness = 1.0 / math.sqrt(probe_embeddings.shape[-1])
    return (
        jnp.einsum(
            "...xqi,...qxs->...ixs",
            derivative_sequence,
            probe_embeddings,
            preferred_element_type=jnp.float32,
        )
        * softmax_sharpness
    )


def value_grads(probabilities, result_cotangent):
    return jnp.einsum(
        "...xqi,...qxs->...ixs", probabilities, result_cotangent, preferred_element_type=jnp.float32
    )


def by_segment(array, segs):
    heads = array.shape[0]
    return jnp.transpose(array.reshape(heads, segs, array.shape[1] // segs), (1, 0, 2))


def per_device(
    tiles,
    cotangent,
    gain,
    query_matrix,
    key_matrix,
    value_matrix,
    w_out,
    query_down_factor,
    query_up_factor,
    value_down_factor,
    value_up_factor,
    valid_count,
):
    highest_precision = lax.Precision.HIGHEST
    entry_number = tiles.shape[1]
    width = tiles.shape[2]
    heads = HEAD_COUNT
    size = width // heads
    step_stride = entry_number // G_DEV
    sparse_selection = entry_number // MIDDLE_DILATION
    segs = entry_number // FINE_SEGMENT0
    valid = valid_count[0]
    level_index = lax.axis_index("seq")
    local_positions = level_index * entry_number + jnp.arange(entry_number, dtype=jnp.int32)
    centered_input, inverse_deviation = layer_normalize(tiles[0])
    normed_input = (centered_input * gain.astype(jnp.float32)).astype(jnp.bfloat16)
    query_lift = jnp.dot(normed_input, query_down_factor, preferred_element_type=jnp.float32)
    value_lift = jnp.dot(normed_input, value_down_factor, preferred_element_type=jnp.float32)
    flat_q = (
        jnp.dot(normed_input, query_matrix, preferred_element_type=jnp.float32)
        + adapter_scale
        * jnp.dot(query_lift, query_up_factor.astype(jnp.float32), precision=highest_precision)
    ).astype(jnp.bfloat16)
    flattened_keys = jnp.dot(normed_input, key_matrix, preferred_element_type=jnp.float32).astype(
        jnp.bfloat16
    )
    flattened_values = (
        jnp.dot(normed_input, value_matrix, preferred_element_type=jnp.float32)
        + adapter_scale
        * jnp.dot(value_lift, value_up_factor.astype(jnp.float32), precision=highest_precision)
    ).astype(jnp.bfloat16)
    flat_da = jnp.dot(cotangent[0], w_out.T, preferred_element_type=jnp.float32).astype(
        jnp.bfloat16
    )
    probe_embeddings = flat_q.reshape(entry_number, heads, size)
    address_embeddings = flattened_keys.reshape(entry_number, heads, size)
    payload_vectors = flattened_values.reshape(entry_number, heads, size)
    attention_gradient = flat_da.reshape(entry_number, heads, size)
    seg_q = probe_embeddings.reshape(segs, FINE_SEGMENT0, heads, size)
    seg_k = address_embeddings.reshape(segs, FINE_SEGMENT0, heads, size)
    seg_v = payload_vectors.reshape(segs, FINE_SEGMENT0, heads, size)
    seg_da = attention_gradient.reshape(segs, FINE_SEGMENT0, heads, size)
    seg_pos = local_positions.reshape(segs, FINE_SEGMENT0)

    def local_sums(item):
        part_q, part_k, part_pos = item
        return jnp.sum(exponentials(part_q, part_k, allowed_keys(part_pos, part_pos, valid)), -1)

    local_total = lax.map(local_sums, (seg_q, seg_k, seg_pos))
    couple_queries = probe_embeddings[::MIDDLE_DILATION]
    couple_keys = address_embeddings[::MIDDLE_DILATION]
    couple_values = payload_vectors[::MIDDLE_DILATION]
    couple_attention_delta = attention_gradient[::MIDDLE_DILATION]
    couple_positions = local_positions[::MIDDLE_DILATION]
    remote_keys, remote_values = partner(
        (flattened_keys[::MIDDLE_DILATION], flattened_values[::MIDDLE_DILATION]), "seq", 0
    )
    remote_positions = jnp.bitwise_xor(level_index, 1) * entry_number + jnp.arange(
        0, entry_number, MIDDLE_DILATION, dtype=jnp.int32
    )
    joined_keys = jnp.concatenate(
        [couple_keys, remote_keys.reshape(sparse_selection, heads, size)], 0
    )
    joined_values = jnp.concatenate(
        [couple_values, remote_values.reshape(sparse_selection, heads, size)], 0
    )
    both_pos = jnp.concatenate([couple_positions, remote_positions], 0)
    couple_exponentials = exponentials(
        couple_queries, joined_keys, allowed_keys(couple_positions, both_pos, valid)
    )
    far_q = probe_embeddings[::step_stride]
    far_da = attention_gradient[::step_stride]
    far_pos = local_positions[::step_stride]
    all_k, all_v = (
        lax.all_gather(flattened_keys[::step_stride], "seq", axis=0, tiled=True),
        lax.all_gather(flattened_values[::step_stride], "seq", axis=0, tiled=True),
    )
    count_all = all_k.shape[0]
    all_k = all_k.reshape(count_all, heads, size)
    all_v = all_v.reshape(count_all, heads, size)
    all_pos = jnp.arange(count_all, dtype=jnp.int32) * step_stride
    far_expo = exponentials(far_q, all_k, allowed_keys(far_pos, all_pos, valid))
    total_sum = jnp.transpose(local_total, (1, 0, 2)).reshape(heads, entry_number)
    total_sum = total_sum.at[:, ::MIDDLE_DILATION].add(jnp.sum(couple_exponentials, -1))
    total_sum = total_sum.at[:, ::step_stride].add(jnp.sum(far_expo, -1))
    seg_total = by_segment(total_sum, segs)

    def local_mix(item):
        part_q, part_k, part_v, part_pos, part_total = item
        expo = exponentials(part_q, part_k, allowed_keys(part_pos, part_pos, valid))
        return value_mixing(weights_of(expo, part_total), part_v)

    mixed_output = lax.map(local_mix, (seg_q, seg_k, seg_v, seg_pos, seg_total)).reshape(
        entry_number, heads, size
    )
    couple_total = total_sum[:, ::MIDDLE_DILATION]
    couple_probabilities = weights_of(couple_exponentials, couple_total)
    mixed_output = mixed_output.at[::MIDDLE_DILATION].add(
        value_mixing(couple_probabilities, joined_values)
    )
    far_total = total_sum[:, ::step_stride]
    far_probs = weights_of(far_expo, far_total)
    mixed_output = mixed_output.at[::step_stride].add(value_mixing(far_probs, all_v))
    attended = mixed_output.astype(jnp.bfloat16)
    row_delta = jnp.sum(attention_gradient.astype(jnp.float32) * attended.astype(jnp.float32), -1).T
    seg_delta = by_segment(row_delta, segs)

    def local_back(item):
        part_q, part_k, part_v, part_pos, part_total, part_delta, part_da = item
        expo = exponentials(part_q, part_k, allowed_keys(part_pos, part_pos, valid))
        probabilities = weights_of(expo, part_total)
        derivative_sequence = score_grads(expo, part_total, part_delta, part_da, part_v)
        return (
            query_gradients(derivative_sequence, part_k),
            key_grads(derivative_sequence, part_q),
            value_grads(probabilities, part_da),
        )

    local_q, local_k, local_v = lax.map(
        local_back, (seg_q, seg_k, seg_v, seg_pos, seg_total, seg_delta, seg_da)
    )
    query_gradient = local_q.reshape(entry_number, heads, size)
    key_gradient = local_k.reshape(entry_number, heads, size)
    value_gradient = local_v.reshape(entry_number, heads, size)
    couple_delta = row_delta[:, ::MIDDLE_DILATION]
    couple_gradients = score_grads(
        couple_exponentials, couple_total, couple_delta, couple_attention_delta, joined_values
    )
    query_gradient = query_gradient.at[::MIDDLE_DILATION].add(
        query_gradients(couple_gradients, joined_keys)
    )
    far_delta = row_delta[:, ::step_stride]
    far_grads = score_grads(far_expo, far_total, far_delta, far_da, all_v)
    query_gradient = query_gradient.at[::step_stride].add(query_gradients(far_grads, all_k))
    pair_kg = key_grads(couple_gradients, couple_queries)
    pair_vg = value_grads(couple_probabilities, couple_attention_delta)
    back_k, value_return = (
        partner(
            pair_kg[sparse_selection:].reshape(sparse_selection, width).astype(jnp.bfloat16),
            "seq",
            0,
        ).astype(jnp.float32),
        partner(
            pair_vg[sparse_selection:].reshape(sparse_selection, width).astype(jnp.bfloat16),
            "seq",
            0,
        ).astype(jnp.float32),
    )
    local_couple_keys = pair_kg[:sparse_selection] + back_k.reshape(sparse_selection, heads, size)
    local_couple_values = pair_vg[:sparse_selection] + value_return.reshape(
        sparse_selection, heads, size
    )
    summed = lax.psum_scatter(
        jnp.concatenate(
            [
                key_grads(far_grads, far_q).reshape(G_DEV * lax.axis_size("seq"), width),
                value_grads(far_probs, far_da).reshape(G_DEV * lax.axis_size("seq"), width),
            ],
            1,
        ).astype(jnp.bfloat16),
        "seq",
        scatter_dimension=0,
        tiled=True,
    ).astype(jnp.float32)
    local_distant_keys = summed[:, :width].reshape(G_DEV, heads, size)
    local_distant_values = summed[:, width:].reshape(G_DEV, heads, size)
    key_gradient = (
        key_gradient.at[::MIDDLE_DILATION]
        .add(local_couple_keys)
        .at[::step_stride]
        .add(local_distant_keys)
    )
    value_gradient = (
        value_gradient.at[::MIDDLE_DILATION]
        .add(local_couple_values)
        .at[::step_stride]
        .add(local_distant_values)
    )
    rounded_queries = query_gradient.astype(jnp.bfloat16).reshape(entry_number, width)
    rounded_keys = key_gradient.astype(jnp.bfloat16).reshape(entry_number, width)
    rounded_values = value_gradient.astype(jnp.bfloat16).reshape(entry_number, width)
    query_return = jnp.dot(rounded_queries, query_up_factor.T, preferred_element_type=jnp.float32)
    value_return = jnp.dot(rounded_values, value_up_factor.T, preferred_element_type=jnp.float32)
    normed_gradient = (
        jnp.dot(rounded_queries, query_matrix.T, preferred_element_type=jnp.float32)
        + jnp.dot(rounded_keys, key_matrix.T, preferred_element_type=jnp.float32)
        + jnp.dot(rounded_values, value_matrix.T, preferred_element_type=jnp.float32)
        + adapter_scale
        * jnp.dot(
            query_return, query_down_factor.astype(jnp.float32).T, precision=highest_precision
        )
        + adapter_scale
        * jnp.dot(
            value_return, value_down_factor.astype(jnp.float32).T, precision=highest_precision
        )
    )
    scaled_scores = normed_gradient * gain.astype(jnp.float32)
    incoming_derivative = inverse_deviation * (
        scaled_scores
        - jnp.mean(scaled_scores, -1, keepdims=True)
        - centered_input * jnp.mean(scaled_scores * centered_input, -1, keepdims=True)
    )
    normed_widened = normed_input.astype(jnp.float32)
    low_rank_couplets = jnp.stack(
        [
            adapter_scale * jnp.dot(query_return.T, normed_widened, precision=highest_precision),
            adapter_scale
            * jnp.dot(
                query_lift.T, rounded_queries.astype(jnp.float32), precision=highest_precision
            ),
            adapter_scale * jnp.dot(value_return.T, normed_widened, precision=highest_precision),
            adapter_scale
            * jnp.dot(
                value_lift.T, rounded_values.astype(jnp.float32), precision=highest_precision
            ),
        ]
    )
    merged_low_rank = lax.psum(low_rank_couplets, ("dp", "seq"))
    softmax_sharpness = 1.0 / math.sqrt(lax.axis_size("dp") * lax.axis_size("seq") * entry_number)
    return (incoming_derivative.astype(jnp.bfloat16)[None], merged_low_rank * softmax_sharpness)


def solution(mesh):
    placed = (
        P("dp", "seq", None),
        P("dp", "seq", None),
        P(),
        P(),
        P(),
        P(),
        P(),
        P(),
        P(),
        P(),
        P(),
        P("dp"),
    )
    return jax.shard_map(
        per_device,
        mesh=mesh,
        in_specs=placed,
        out_specs=(P("dp", "seq", None), P()),
        check_vma=False,
    )
```

profile of v0, /device:TPU:1, one launch (start us, length us, event | category | flops | bytes accessed | tf_op | source)
XLA Modules:
  0.0 723.4 jit_solution(5700718260852150478)
XLA Ops:
  14.0 3.2 collective-permute-start
  31.4 3.5 convolution_convert_fusion
  37.2 3.7 slice.82
  40.9 10.0 %slice.80 = bf16[128,16,48]{0,2,1:T(8,128)(2,1)} slice(bf16[512,16,48]{0,2,1:T(8,128)(2,1)} %bitcast.174), slice={[0:512:4], [0:16:1], [0:48:1]} | slice | bytes 393216 | tf_op jit(solution)/shard_map/slice | solution.py:169
  60.8 3.7 slice.73
  64.5 10.0 %slice.69 = bf16[128,16,48]{0,2,1:T(8,128)(2,1)} slice(bf16[512,16,48]{0,2,1:T(8,128)(2,1)} %bitcast.179), slice={[0:512:4], [0:16:1], [0:48:1]} | slice | bytes 393216 | tf_op jit(solution)/shard_map/slice | solution.py:166
  79.7 9.2 %slice.70 = bf16[128,16,48]{0,2,1:T(8,128)(2,1)} slice(bf16[512,16,48]{0,2,1:T(8,128)(2,1)S(1)} %bitcast.170), slice={[0:512:4], [0:16:1], [0:48:1]} | slice | bytes 393216 | tf_op jit(solution)/shard_map/slice | solution.py:167
  88.9 40.9 %all_gather.6 = bf16[512,768]{1,0:T(8,128)(2,1)} all-gather(bf16[16,768]{1,0:T(8,128)(2,1)} %slice.74), channel_id=1, replica_groups=mesh['dp'=8,'seq'=32] {'seq'}, dimensions={0}, use_global_device_ids=true | all-gather | bytes 811008 | tf_op jit(solution)/shard_map/all_gather | solution.py:191
  131.2 10.0 %slice.75 = bf16[128,16,48]{0,2,1:T(8,128)(2,1)} slice(bf16[512,16,48]{0,2,1:T(8,128)(2,1)} %bitcast.185), slice={[0:512:4], [0:16:1], [0:48:1]} | slice | bytes 393216 | tf_op jit(solution)/shard_map/slice | solution.py:168
  141.3 35.7 %all_gather.7 = bf16[512,768]{1,0:T(8,128)(2,1)} all-gather(bf16[16,768]{1,0:T(8,128)(2,1)} %slice.78), channel_id=1, replica_groups=mesh['dp'=8,'seq'=32] {'seq'}, dimensions={0}, use_global_device_ids=true | all-gather | bytes 811008 | tf_op jit(solution)/shard_map/all_gather | solution.py:192
  184.0 11.8 %fusion.1 = (f32[16,512]{1,0:T(8,128)}, f32[16,512,512]{1,2,0:T(8,128)}) fusion(pred[512,512]{0,1:T(8,128)(4,1)} %compare_or_fusion, bf16[512,16,48]{0,2,1:T(8,128)(2,1)} %bitcast.180, bf16[512,16,48]{0,2,1:T(8,128)(2,1)} %bitcast.171), kind=kOutput, calls=%fused_computation.13 | convolution fusion | flops 415227904 | bytes 18644992 | tf_op jit(solution)/shard_map/while/body/eval_jaxpr/...fou,...iou->...ofi/dot_general | solution.py:36
  200.4 3.6 fusion.7
  223.0 3.1 convolution_bitcast_fusion.1
  228.6 9.0 %fusion.20 = f32[512,16,48]{0,2,1:T(8,128)} fusion(bf16[512,16,48]{0,2,1:T(8,128)(2,1)} %bitcast.186, f32[16,512,512]{1,2,0:T(8,128)} %get-tuple-element.61, f32[16,512]{1,0:T(8,128)} %copy.136, pred[512,512]{0,1:T(8,128)(4,1)} %compare_or_fusion), kind=kOutput, calls=%fused_computation.44 | convolution fusion | flops 419430400 | bytes 19431424 | tf_op jit(solution)/shard_map/while/body/eval_jaxpr/...fcz,...zfx->...cfx/dot_general | solution.py:52
  237.6 4.7 copy.142
  242.3 16.3 %scatter_fusion.2 = f32[512,16,48]{2,1,0:T(8,128)} fusion(f32[512,16,48]{2,1,0:T(8,128)} %copy.142, s32[128]{0:T(128)} %multiply_bitcast_fusion.3, f32[128,16,48]{2,1,0:T(8,128)} %copy.143), kind=kCustom, calls=%fused_computation.2 | custom fusion | flops 98304 | bytes 1180160 | tf_op jit(solution)/shard_map/scatter-add | solution.py:214
  261.2 3.5 copy.147
  271.6 3.3 convolution_bitcast_fusion
  287.7 9.4 %multiply_convert_fusion = bf16[16,512,512]{1,2,0:T(8,128)(2,1)S(1)} fusion(bf16[512,16,48]{0,2,1:T(8,128)(2,1)S(1)} %bitcast.177, bf16[512,16,48]{0,2,1:T(8,128)(2,1)S(1)} %bitcast.187, f32[16,512]{1,0:T(8,128)S(1)} %bitcast.198, f32[16,512]{1,0:T(8,128)S(1)} %copy-done.33, f32[16,512,512]{1,2,0:T(8,128)} %get-tuple-element.61, ...), kind=kOutput, calls=%fused_computation.10 | convolution fusion | flops 427819008 | bytes 27066368 | tf_op jit(solution)/shard_map/while/body/eval_jaxpr/...fou,...iou->...ofi/dot_general | solution.py:58
  297.1 3.7 multiply_bitcast_fusion
  304.8 4.7 copy.153
  309.5 16.2 %scatter_fusion.4 = f32[512,16,48]{2,1,0:T(8,128)} fusion(f32[512,16,48]{2,1,0:T(8,128)} %copy.153, s32[128]{0:T(128)S(1)} %copy-done.35, f32[128,16,48]{2,1,0:T(8,128)} %copy.154), kind=kCustom, calls=%fused_computation.4 | custom fusion | flops 98304 | bytes 1180160 | tf_op jit(solution)/shard_map/scatter-add | solution.py:245
  342.7 9.0 %fusion.23 = f32[512,16,48]{0,2,1:T(8,128)} fusion(bf16[512,16,48]{0,2,1:T(8,128)(2,1)} %bitcast.176, f32[16,512,512]{1,2,0:T(8,128)} %get-tuple-element.61, f32[16,512]{1,0:T(8,128)} %copy.136, pred[512,512]{0,1:T(8,128)(4,1)} %compare_or_fusion), kind=kOutput, calls=%fused_computation.45 | convolution fusion | flops 419430400 | bytes 19431424 | tf_op jit(solution)/shard_map/while/body/eval_jaxpr/...xqi,...qxs->...ixs/dot_general | solution.py:96
  355.0 4.9 copy.160
  359.9 4.7 copy.165
  374.8 16.3 %scatter_fusion.6 = f32[512,16,48]{2,1,0:T(8,128)} fusion(f32[512,16,48]{2,1,0:T(8,128)} %copy.160, s32[128]{0:T(128)} %multiply_bitcast_fusion.3, f32[128,16,48]{2,1,0:T(8,128)} %copy.161), kind=kCustom, calls=%fused_computation.6 | custom fusion | flops 98304 | bytes 1180160 | tf_op jit(solution)/shard_map/scatter-add | solution.py:285
  391.1 16.2 %scatter_fusion.8 = f32[512,16,48]{2,1,0:T(8,128)} fusion(f32[512,16,48]{2,1,0:T(8,128)} %copy.165, s32[128]{0:T(128)S(1)} %copy-done.36, f32[128,16,48]{2,1,0:T(8,128)} %copy.166), kind=kCustom, calls=%fused_computation.8 | custom fusion | flops 98304 | bytes 1180160 | tf_op jit(solution)/shard_map/scatter-add | solution.py:291
  407.3 43.5 %reduce-scatter.4.cloned.1.call-done = bf16[16,1536]{1,0:T(8,128)(2,1)} async-done(((bf16[512,1536]{1,0:T(8,128)(2,1)}), bf16[16,1536]{1,0:T(8,128)(2,1)}) %reduce-scatter.4.cloned.1.call-update) | async-done | bytes 49168
  460.2 3.3 fusion.62
  469.8 3.3 fusion.61
  474.2 4.4 fusion.53
  480.0 234.9 %all-reduce.2.cloned.1.call-done = f32[4,8,768]{2,1,0:T(8,128)} async-done(((f32[4,8,768]{2,1,0:T(8,128)}), f32[4,8,768]{2,1,0:T(8,128)}) %all-reduce.2.cloned.1.call-update) | async-done | bytes 98320 | tf_op jit(solution)/shard_map/psum | solution.py:334
  (189 shorter events, 148.5 us)
Async XLA Ops:
  7.2 48.8 %copy-start = (bf16[768,768]{1,0:T(8,128)(2,1)S(1)}, bf16[768,768]{1,0:T(8,128)(2,1)}, u32[]{:S(2)}) copy-start(bf16[768,768]{1,0:T(8,128)(2,1)} %param.15) | copy-start | bytes 3538948
  7.2 3.8 copy-start.1
  7.2 443.6 %reduce-scatter.4.cloned.1.call-start = ((), (), s32[]{:S(2)}) async-start(), calls=%async_computation.2 | async-start | bytes 1622016
  7.2 4.3 copy-start.38
  12.3 5.9 copy-start.11
  14.0 6.3 copy-start.29
  14.0 184.7 %collective-permute-start = (bf16[128,768]{1,0:T(8,128)(2,1)}, bf16[128,768]{1,0:T(8,128)(2,1)}, u32[]{:S(2)}, u32[]{:S(2)}) collective-permute-start(bf16[128,768]{1,0:T(8,128)(2,1)} %slice.71), channel_id=1, source_target_pairs={{0,1},{1,0},{2,3},{3,2},{4,5},{5,4},{6,7},{7,6},{8,9},{9,8},{10,11... | collective-permute-start | bytes 589832 | tf_op jit(solution)/shard_map/ppermute | solution.py:19
  21.2 6.9 copy-start.6
  22.9 198.3 %collective-permute-start.1 = (bf16[128,768]{1,0:T(8,128)(2,1)}, bf16[128,768]{1,0:T(8,128)(2,1)}, u32[]{:S(2)}, u32[]{:S(2)}) collective-permute-start(bf16[128,768]{1,0:T(8,128)(2,1)} %slice.76), channel_id=1, source_target_pairs={{0,1},{1,0},{2,3},{3,2},{4,5},{5,4},{6,7},{7,6},{8,9},{9,8},{10,11... | collective-permute-start | bytes 589832 | tf_op jit(solution)/shard_map/ppermute | solution.py:19
  31.4 48.4 %copy-start.2 = (bf16[512,768]{0,1:T(8,128)(2,1)}, bf16[512,768]{0,1:T(8,128)(2,1)S(1)}, u32[]{:S(2)}) copy-start(bf16[512,768]{0,1:T(8,128)(2,1)S(1)} %copy.128) | copy-start | bytes 2359300
  276.4 4.0 copy-start.16
  284.3 3.4 copy-start.4
  284.3 3.4 copy-start.12
  284.3 3.4 copy-start.18
  284.3 3.4 copy-start.22
  287.7 9.4 %copy-start.5 = (bf16[512,768]{0,1:T(8,128)(2,1)S(1)}, bf16[512,768]{0,1:T(8,128)(2,1)}, u32[]{:S(2)}) copy-start(bf16[512,768]{0,1:T(8,128)(2,1)} %copy.129) | copy-start | bytes 2359300
  297.1 3.7 copy-start.3
  304.8 4.7 copy-start.35
  304.8 20.9 %copy-start.34 = (s32[16]{0:T(128)S(1)}, s32[16]{0:T(128)}, u32[]{:S(2)}) copy-start(s32[16]{0:T(128)} %multiply_bitcast_fusion.2) | copy-start | bytes 196
  332.2 3.8 copy-start.7
  332.2 3.8 copy-start.15
  335.9 30.5 %collective-permute-start.3 = (bf16[128,768]{0,1:T(8,128)(2,1)}, bf16[128,768]{0,1:T(8,128)(2,1)}, u32[]{:S(2)}, u32[]{:S(2)}) collective-permute-start(bf16[128,768]{0,1:T(8,128)(2,1)} %bitcast.35), channel_id=1, source_target_pairs={{0,1},{1,0},{2,3},{3,2},{4,5},{5,4},{6,7},{7,6},{8,9},{9,8},{10,11... | collective-permute-start | bytes 589832 | tf_op jit(solution)/shard_map/ppermute | solution.py:19
  339.9 374.9 %all-reduce.2.cloned.1.call-start = ((), (), s32[]{:S(2)}) async-start(), calls=%async_computation.1 | async-start | bytes 196608 | tf_op jit(solution)/shard_map/psum | solution.py:334
  342.7 9.0 %copy-start.21 = (f32[512,8]{0,1:T(8,128)S(1)}, f32[512,8]{0,1:T(8,128)}, u32[]{:S(2)}) copy-start(f32[512,8]{0,1:T(8,128)} %copy-done.20) | copy-start | bytes 49156
  354.7 16.1 %collective-permute-start.2 = (bf16[128,768]{0,1:T(8,128)(2,1)}, bf16[128,768]{0,1:T(8,128)(2,1)}, u32[]{:S(2)}, u32[]{:S(2)}) collective-permute-start(bf16[128,768]{0,1:T(8,128)(2,1)} %bitcast.25), channel_id=1, source_target_pairs={{0,1},{1,0},{2,3},{3,2},{4,5},{5,4},{6,7},{7,6},{8,9},{9,8},{10,11... | collective-permute-start | bytes 589832 | tf_op jit(solution)/shard_map/ppermute | solution.py:19
  364.6 6.1 copy-start.8
  372.5 18.7 %copy-start.36 = (s32[128]{0:T(128)S(1)}, s32[128]{0:T(128)}, u32[]{:S(2)}) copy-start(s32[128]{0:T(128)} %multiply_bitcast_fusion.3) | copy-start | bytes 1540
  469.8 3.7 copy-start.23
  469.8 3.7 copy-start.24
  469.8 3.7 copy-start.25
  474.1 4.4 copy-start.27
  474.2 4.4 copy-start.32
  (13 other events, 27.3 us)
Sparse Core Ops, SparseCore 0:
  340.1 110.6 reduce-scatter.3
  474.3 240.5 all-reduce.1
where the time goes:
time: 731 us; the launch traced here: 723 us
  waiting for transfers between devices  278 us (38%)
  local copies, waits for them, and re-layouts  141 us (19%)
  other arithmetic  104 us (14%)
  matrix products  104 us (14%)
  blocking collectives  76.6 us (10%)
  between operations  15.4 us (2%)
    psum x1, waiting for transfers between devices, per_device(): merged_low_rank = lax.psum(low_rank_couplets, ('dp', 'seq'))  235 us
    unnamed x3, waiting for transfers between devices  43.5 us
    all_gather x1, blocking collectives, per_device(): lax.all_gather(flattened_keys[::step_stride], 'seq', axis=0, tiled=True)  40.9 us
    all_gather x1, blocking collectives, per_device(): lax.all_gather(flattened_values[::step_stride], 'seq', axis=0, tiled=True)  35.7 us
    scatter-add x2, other arithmetic, per_device(): key_gradient = key_gradient.at[::MIDDLE_DILATION].add(local_couple_keys)....  18.7 us
    scatter-add x2, other arithmetic, per_device(): value_gradient = value_gradient.at[::MIDDLE_DILATION].add(local_couple_va...  18.6 us
    dot_general x3, matrix products, exponentials(): jnp.einsum('...fou,...iou->...ofi', probe_embeddings, address_embeddings,...  18 us
    scatter-add x1, other arithmetic, per_device(): mixed_output.at[::MIDDLE_DILATION]  16.3 us
  transfers between devices with their start and end apart: 6, of which 2 were waited for; matrix products, arithmetic and copies ran while one was open for 28% of the time, Pallas kernels for 0%

commit v1 on v0

v1 whole, which is shorter than its diff:
```python
import math

import jax
import jax.numpy as jnp
from jax import lax
from jax.experimental import pallas as pl
from jax.experimental.pallas import tpu as pltpu
from jax.sharding import PartitionSpec as P

T = 512
D = 768
H = 16
W = 48
R = 8
PAIR = 128
FAR = 16
SEQ = 32
DP = 8
CHIPS = 16
GROUPS = 2
SLICES = 12
PER = 8
EPS = 1e-5
LOG2E = math.log2(math.e)
SHARP = 1.0 / math.sqrt(W)
LN2 = math.log(2.0)
MESH = pl.DeviceIdType.MESH
f32 = jnp.float32
bf16 = jnp.bfloat16
VMEM_LIMIT = 56 * 1024 * 1024


def iota(shape, axis):
    return lax.broadcasted_iota(jnp.int32, shape, axis)


def dot(a, b):
    return jnp.dot(a, b, preferred_element_type=f32)


def dot_nt(a, b):
    return lax.dot_general(a, b, (((1,), (1,)), ((), ())), preferred_element_type=f32)


def place_of(row):
    return (row % 16) * 32 + ((row // 16) % 8) * 4 + row // 128


def order_matrix():
    return jnp.where(place_of(iota((T, T), 0)) == iota((T, T), 1), 1.0, 0.0).astype(bf16)


def halves(value):
    upper = value.astype(bf16)
    lower = (value - upper.astype(f32)).astype(bf16)
    return upper, lower


def normalize(x):
    center = x - jnp.mean(x, -1, keepdims=True)
    inverse = lax.rsqrt(jnp.mean(center * center, -1, keepdims=True) + EPS)
    return center * inverse, inverse


def window(hh):
    low = W * hh
    first = low // 128
    last = (low + W - 1) // 128
    return first * 128, (last - first + 1) * 128, low - first * 128


def lane_mask(width, off):
    lane = iota((1, width), 1)
    return jnp.where((lane >= off) & (lane < off + W), 1.0, 0.0).astype(bf16)


def pad_rows(block, off, width):
    parts = []
    if off:
        parts.append(jnp.zeros((off, block.shape[1]), block.dtype))
    parts.append(block)
    rest = width - off - block.shape[0]
    if rest:
        parts.append(jnp.zeros((rest, block.shape[1]), block.dtype))
    return jnp.concatenate(parts, 0)


def down_rows(qd_ref, vd_ref):
    return jnp.concatenate(
        [qd_ref[...].astype(f32), vd_ref[...].astype(f32), jnp.zeros((112, D), f32)], 0
    ).astype(bf16)


def up_padded(u_ref, at):
    return pad_rows(u_ref[...].astype(f32), at, 128).astype(bf16)


def layer_kernel(
    valid_ref, tiles_ref, cot_ref, gain_ref, wq_ref, wk_ref, wv_ref, wo_ref,
    qd_ref, qu_ref, vd_ref, vu_ref,
    out_ref, merged_ref,
    xhat_s, scale_s, normed_s, lift_s, q_ref, k_ref, v_ref, qt_ref, kt_ref, vt_ref, dat_ref,
    skv_ref, sqd_ref,
    e0, e1, mask0, mask1, tot, mix, dlt, dapt, dap, dqt, dq1t, dk, dv,
    k1, v1, k1t, v1t, dk1, dv1, gsend, gback,
    kv, qda, fe, send2, recv2, send3, recv3, skvg, sdq, rkvg, rdq,
    part, one, total, two, done,
    s_kv, r_kv, s_qd, r_qd, s_pair, r_pair, s_2, r_2, s_3, r_3, s_4, r_4, s_5, r_5, s_g, r_g,
    s_6, r_6, s_7, r_7, s_8, r_8,
):
    dp = lax.axis_index("dp")
    me = lax.axis_index("seq")
    chip = me // 2
    core = me % 2
    mate = chip * 2 + (1 - core)
    mine = me % 16
    half = me // 16
    plane = dp * 2 + half
    valid = valid_ref[0]

    def near_peer(j):
        return {"seq": half * 16 + (mine + j) % 16}

    def across_peer(j):
        other = (plane + j) % 16
        return {"dp": other // 2, "seq": (other % 2) * 16 + mine}

    barrier = pltpu.get_barrier_semaphore()

    def greet(j, carry):
        pl.semaphore_signal(
            barrier, inc=1, device_id={"seq": (me + j) % SEQ}, device_id_type=MESH
        )
        return carry

    def greet_across(j, carry):
        pl.semaphore_signal(barrier, inc=1, device_id=across_peer(j), device_id_type=MESH)
        return carry

    lax.fori_loop(1, SEQ, greet, 0)
    lax.fori_loop(1, 16, greet_across, 0)

    def remote_to(src, dst, send, recv, peer):
        return pltpu.make_async_remote_copy(
            src_ref=src, dst_ref=dst, send_sem=send, recv_sem=recv,
            device_id=peer, device_id_type=MESH,
        )

    def remote(src, dst, send, recv, peer):
        return remote_to(src, dst, send, recv, {"seq": peer})

    def drain(ref, sem):
        pltpu.make_async_copy(ref, ref, sem).wait()

    order = order_matrix()
    x = dot(order, tiles_ref[0])
    cot = dot(order, cot_ref[0]).astype(bf16)
    xhat, inverse_dev = normalize(x)
    xhat_s[...] = xhat
    scale_s[...] = jnp.broadcast_to(inverse_dev, (T, 128))
    normed = (xhat * gain_ref[...].astype(f32)).astype(bf16)
    normed_s[...] = normed
    down = down_rows(qd_ref, vd_ref)
    uq = up_padded(qu_ref, 0)
    uv = up_padded(vu_ref, R)
    lift = dot_nt(normed, down)
    both = jnp.concatenate(halves(lift), 1)
    lift_s[...] = lift.T[: 2 * R]
    q = dot(normed, wq_ref[...]) + 2.0 * dot(both, jnp.concatenate([uq, uq], 0))
    q = (q * (SHARP * LOG2E)).astype(bf16)
    q_ref[...] = q
    qt_ref[...] = q.T
    k = dot(normed, wk_ref[...]).astype(bf16)
    k_ref[...] = k
    kt_ref[...] = k.T
    v = (dot(normed, wv_ref[...]) + 2.0 * dot(both, jnp.concatenate([uv, uv], 0))).astype(bf16)
    v_ref[...] = v
    vt_ref[...] = v.T
    da = dot_nt(cot, wo_ref[...]).astype(bf16)
    dat_ref[...] = da.T
    gap = jnp.zeros((FAR, 64 - W), f32)
    qf, kf, vf, df = (rows[:FAR].astype(f32) for rows in (q, k, v, da))
    for h in range(H):
        cut = slice(W * h, W * h + W)
        skv_ref[h] = jnp.concatenate([kf[:, cut], gap, vf[:, cut], gap], 1).astype(bf16)
        sqd_ref[h] = jnp.concatenate([qf[:, cut], gap, df[:, cut], gap], 1).astype(bf16)

    pl.semaphore_wait(barrier, SEQ - 1 + 15)

    mine_rows = pl.ds(pl.multiple_of(core * 256 + chip * FAR, FAR), FAR)

    def slot(c):
        return pl.ds(pl.multiple_of(c * FAR, FAR), FAR)

    def send_same(j, carry):
        there = (chip + j) % CHIPS
        remote(skv_ref.at[there], kv.at[mine_rows], s_kv, r_kv, there * 2 + core).start()
        remote(sqd_ref.at[there], qda.at[slot(chip)], s_qd, r_qd, there * 2 + core).start()
        return carry

    def send_other(j, carry):
        there = (chip + j) % CHIPS
        remote(skv_ref.at[there], kv.at[mine_rows], s_kv, r_kv, there * 2 + (1 - core)).start()
        return carry

    lax.fori_loop(1, CHIPS, send_same, 0)
    lax.fori_loop(0, CHIPS, send_other, 0)
    pltpu.make_async_copy(skv_ref.at[chip], kv.at[mine_rows], r_kv).start()
    pltpu.make_async_copy(sqd_ref.at[chip], qda.at[slot(chip)], r_qd).start()

    near = pl.ds(0, PAIR)
    away = pl.ds(PAIR, PAIR)
    pair_copies = [
        remote(k_ref.at[near], k1.at[away], s_pair.at[0], r_pair.at[0], mate),
        remote(v_ref.at[near], v1.at[away], s_pair.at[1], r_pair.at[1], mate),
        remote(kt_ref.at[:, near], k1t.at[:, away], s_pair.at[2], r_pair.at[2], mate),
        remote(vt_ref.at[:, near], v1t.at[:, away], s_pair.at[3], r_pair.at[3], mate),
    ]
    for copy in pair_copies:
        copy.start()
    k1[near] = k_ref[near]
    v1[near] = v_ref[near]
    k1t[:, near] = kt_ref[:, near]
    v1t[:, near] = vt_ref[:, near]

    row = iota((T, T), 0)
    col = iota((T, T), 1)
    open0 = (me * T + place_of(row) < valid) | (row == col)
    mask0[...] = jnp.where(open0, jnp.inf, 0.0).astype(bf16)
    mask1[near] = mask0[near, near]
    row = iota((PAIR, PAIR), 0)
    mask1[away] = jnp.where(mate * T + place_of(row) < valid, jnp.inf, 0.0).astype(bf16)
    dk[...] = jnp.zeros_like(dk)
    dv[...] = jnp.zeros_like(dv)
    dk1[...] = jnp.zeros_like(dk1)
    dv1[...] = jnp.zeros_like(dv1)

    def place(g, hh):
        base, width, off = window(hh)
        lanes = pl.ds(pl.multiple_of(g * 384 + base, 128), width)
        rows = pl.ds(pl.multiple_of(g * 384 + W * hh, 16), W)
        return lanes, rows, width, off

    def forward(g, store, mask, keys, values_t, asks_t, out):
        totals = []
        for hh in range(PER):
            lanes, rows, width, off = place(g, hh)
            ask = pad_rows(asks_t(rows), off, width)
            expo = jnp.exp2(dot(keys(lanes), ask)).astype(bf16)
            expo = jnp.minimum(expo, mask[...])
            store[g * PER + hh] = expo
            value = values_t(rows)
            ones = jnp.ones((16, value.shape[1]), bf16)
            mixed = dot(jnp.concatenate([value, ones], 0), expo)
            totals.append(mixed[W : W + 1])
            out(rows, mixed[:W])
        return jnp.concatenate(totals, 0)

    def eight(g):
        return pl.ds(pl.multiple_of(g * PER, PER), PER)

    def forward0(g, carry):
        def put(rows, value):
            mix[rows, :] = value

        tot[eight(g), :] = forward(
            g, e0, mask0, lambda l: k_ref[:, l], lambda r: vt_ref[r, :], lambda r: qt_ref[r, :], put
        )
        return carry

    def forward1(g, carry):
        def put(rows, value):
            mix[rows, near] += value

        tot[eight(g), near] += forward(
            g, e1, mask1, lambda l: k1[:, l], lambda r: v1t[r, :], lambda r: qt_ref[r, near], put
        )
        return carry

    lax.fori_loop(0, 1, forward0, 0)

    drain(kv, r_kv)
    drain(qda, r_qd)
    lane = iota((1, 128), 1)
    low = jnp.where(lane < 64, 1.0, 0.0).astype(bf16)
    high = jnp.where(lane >= 64, 1.0, 0.0).astype(bf16)
    i2 = iota((256, T), 0)
    j2 = iota((256, T), 1)
    j2_pos = ((j2 % 256) // FAR * 2 + j2 // 256) * T + (j2 % FAR) * 32
    open2 = (j2_pos < valid) | (j2 == core * 256 + i2)
    far_expo = jnp.exp2(dot_nt(qda[...], kv[...] * low))
    far_expo = jnp.where(open2, far_expo, 0.0).astype(bf16)
    fe[...] = far_expo
    first_lane = jnp.where(lane == 0, 1.0, 0.0).astype(bf16)
    far_mixed = dot(far_expo, kv[...] * high + first_lane)
    far_r = jnp.sum(
        jnp.where(lane >= 64, qda[...].astype(f32) * far_mixed, 0.0), 1, keepdims=True
    )
    far_t = far_mixed[:, 0:1]
    send2[...] = jnp.where(lane == chip, far_t, 0.0) + jnp.where(lane == 64 + chip, far_r, 0.0)

    def send_totals(j, carry):
        there = (chip + j) % CHIPS
        remote(send2.at[slot(there)], recv2.at[slot(chip)], s_2, r_2, there * 2 + core).start()
        return carry

    lax.fori_loop(1, CHIPS, send_totals, 0)
    pltpu.make_async_copy(send2.at[slot(chip)], recv2.at[slot(chip)], r_2).start()

    lax.fori_loop(1, 2, forward0, 0)
    for copy in pair_copies:
        copy.wait()
    lax.fori_loop(0, GROUPS, forward1, 0)

    drain(recv2, r_2)
    gathered = recv2[pl.ds(0, FAR)]
    for c in range(1, CHIPS):
        gathered = gathered + recv2[pl.ds(c * FAR, FAR)]
    turned = jnp.concatenate([gathered, jnp.zeros((PAIR - FAR, 128), f32)], 0).T
    tot[:, near] += turned[:H]
    inverse = 1.0 / tot[...]
    tot[...] = inverse
    far_sums = jnp.concatenate([turned[64 : 64 + H], jnp.zeros((H, T - PAIR), f32)], 1)
    dlt[...] = far_sums * inverse * inverse
    for h in range(H):
        rows = pl.ds(W * h, W)
        this = tot[h : h + 1, :]
        scaled = (dat_ref[rows, :].astype(f32) * this).astype(bf16)
        dapt[rows, :] = scaled
        own = jnp.sum(scaled.astype(f32) * mix[rows, :], 0, keepdims=True)
        dlt[h : h + 1, :] += own * this
    filler = jnp.zeros((64 - H, 128), f32)
    send3[...] = jnp.concatenate([tot[:, near], filler, dlt[:, near], filler], 0).T[:FAR]

    def send_scales(j, carry):
        there = (chip + j) % CHIPS
        remote(send3, recv3.at[slot(chip)], s_3, r_3, there * 2 + core).start()
        return carry

    lax.fori_loop(1, CHIPS, send_scales, 0)
    pltpu.make_async_copy(send3, recv3.at[slot(chip)], r_3).start()
    dap[...] = dapt[...].T

    def backward(g, store, values, keys_t, grads, grads_t, deltas, out_q, out_v):
        for hh in range(PER):
            lanes, rows, width, off = place(g, hh)
            expo = store[g * PER + hh]
            dprob = dot(values(lanes), pad_rows(grads_t(rows), off, width))
            dscore = expo * (dprob - deltas(hh)).astype(bf16)
            store[g * PER + hh] = dscore
            out_q[rows, :] = dot(keys_t(rows), dscore)
            out_v[:, lanes] += dot(expo, grads(lanes) * lane_mask(width, off))

    def key_side(g, store, asks, out_k):
        for hh in range(PER):
            lanes, rows, width, off = place(g, hh)
            out_k[:, lanes] += dot(store[g * PER + hh], asks(lanes) * lane_mask(width, off))

    def backward0(g, carry):
        deltas = dlt[eight(g), :]
        backward(
            g, e0, lambda l: v_ref[:, l], lambda r: kt_ref[r, :], lambda l: dap[:, l],
            lambda r: dapt[r, :], lambda hh: deltas[hh : hh + 1], dqt, dv,
        )
        return carry

    def backward1(g, carry):
        deltas = dlt[eight(g), near]
        backward(
            g, e1, lambda l: v1[:, l], lambda r: k1t[r, :], lambda l: dap[near, l],
            lambda r: dapt[r, near], lambda hh: deltas[hh : hh + 1], dq1t, dv1,
        )
        key_side(g, e1, lambda l: q_ref[near, l], dk1)
        return carry

    def keys0(g, carry):
        key_side(g, e0, lambda l: q_ref[:, l], dk)
        return carry

    lax.fori_loop(0, GROUPS, backward1, 0)
    gsend[0] = dk1[away].astype(bf16)
    gsend[1] = dv1[away].astype(bf16)
    grad_copy = remote(gsend, gback, s_g, r_g, mate)
    grad_copy.start()
    lax.fori_loop(0, 1, backward0, 0)

    drain(recv3, r_3)
    scales = recv3[...]
    far_inv = jnp.sum(jnp.where(lane == chip, scales, 0.0), 1, keepdims=True)
    far_del = jnp.sum(jnp.where(lane == 64 + chip, scales, 0.0), 1, keepdims=True)
    far_grads = jnp.where(lane >= 64, qda[...].astype(f32) * far_inv, 0.0).astype(bf16)
    far_back = fe[...].astype(f32)
    far_ds = far_back * (dot_nt(far_grads, kv[...] * high) - far_del)
    sdq[...] = dot(far_ds.astype(bf16), kv[...] * low).astype(bf16)
    skvg[...] = (
        dot(far_ds.T.astype(bf16), qda[...] * low) + dot(far_back.T.astype(bf16), far_grads)
    ).astype(bf16)

    def return_same(j, carry):
        there = (chip + j) % CHIPS
        block = pl.ds(pl.multiple_of(core * 256 + there * FAR, FAR), FAR)
        remote(skvg.at[block], rkvg.at[mine_rows], s_4, r_4, there * 2 + core).start()
        remote(sdq.at[slot(there)], rdq.at[slot(chip)], s_5, r_5, there * 2 + core).start()
        return carry

    def return_other(j, carry):
        there = (chip + j) % CHIPS
        block = pl.ds(pl.multiple_of((1 - core) * 256 + there * FAR, FAR), FAR)
        remote(skvg.at[block], rkvg.at[mine_rows], s_4, r_4, there * 2 + (1 - core)).start()
        return carry

    lax.fori_loop(1, CHIPS, return_same, 0)
    lax.fori_loop(0, CHIPS, return_other, 0)
    pltpu.make_async_copy(skvg.at[mine_rows], rkvg.at[mine_rows], r_4).start()
    pltpu.make_async_copy(sdq.at[slot(chip)], rdq.at[slot(chip)], r_5).start()

    lax.fori_loop(1, 2, backward0, 0)

    grad_copy.wait()
    drain(rkvg, r_4)
    drain(rdq, r_5)
    keys_back, values_back, asks_back = [], [], []
    for h in range(H):
        here = rkvg[pl.ds(h * FAR, FAR)].astype(f32) + rkvg[pl.ds(256 + h * FAR, FAR)].astype(f32)
        keys_back.append(here[:, :W])
        values_back.append(here[:, 64 : 64 + W])
        asks_back.append(rdq[pl.ds(h * FAR, FAR)].astype(f32)[:, :W])
    few = pl.ds(0, FAR)
    dv[near] += dv1[near] + gback[1].astype(f32)
    dv[few] += jnp.concatenate(values_back, 1)
    dk[near] = dk1[near] + gback[0].astype(f32)
    dk[few] += jnp.concatenate(keys_back, 1)
    dqt[:, near] += dq1t[...]
    gq = dqt[...].T
    gq = jnp.concatenate([gq[:FAR] + jnp.concatenate(asks_back, 1), gq[FAR:]], 0)
    gq = (gq * SHARP).astype(bf16)
    gv = dv[...].astype(bf16)
    back = dot_nt(gq, uq) + dot_nt(gv, uv)
    back_both = jnp.concatenate(halves(back), 1)
    bu, bl = halves(back.T[: 2 * R])
    lu, ll = halves(lift_s[...])
    from_back = dot(jnp.concatenate([bu, bl], 0), normed_s[...])
    from_back = 2.0 * (from_back[:16] + from_back[16:])
    lifts = jnp.concatenate([lu, ll], 0)
    from_q = dot(lifts, gq)
    from_q = 2.0 * (from_q[:R] + from_q[16 : 16 + R])
    from_v = dot(lifts, gv)
    from_v = 2.0 * (from_v[R:16] + from_v[16 + R : 32])
    pairs = [
        jnp.concatenate([from_back[:R], from_q], 0), jnp.concatenate([from_back[R:16], from_v], 0)
    ]
    for p in range(2):
        for c in range(6):
            part[p * 6 + c] = pairs[p][:, 128 * c : 128 * c + 128].astype(bf16)

    def first(j, carry):
        there = (mine + j) % 16

        @pl.when(there < SLICES)
        def _():
            remote_to(part.at[there], one.at[mine], s_6, r_6, near_peer(j)).start()

        return carry

    lax.fori_loop(1, 16, first, 0)

    @pl.when(mine < SLICES)
    def _():
        pltpu.make_async_copy(part.at[mine], one.at[mine], r_6).start()

    lax.fori_loop(0, GROUPS, keys0, 0)

    @pl.when(mine < SLICES)
    def _():
        drain(one, r_6)
        total[0] = jnp.sum(one[...].astype(f32), 0).astype(bf16)

        def second(j, carry):
            remote_to(total.at[0], two.at[plane], s_7, r_7, across_peer(j)).start()
            return carry

        lax.fori_loop(1, 16, second, 0)
        pltpu.make_async_copy(total.at[0], two.at[plane], r_7).start()

    gk = (dk[...] * LN2).astype(bf16)
    grad = (
        dot_nt(gq, wq_ref[...])
        + dot_nt(gk, wk_ref[...])
        + dot_nt(gv, wv_ref[...])
        + 2.0 * dot(back_both, jnp.concatenate([down, down], 0))
    )
    s = grad * gain_ref[...].astype(f32)

    @pl.when(mine < SLICES)
    def _():
        drain(two, r_7)
        both_sum = jnp.sum(two[...].astype(f32), 0) * (1.0 / math.sqrt(SEQ * DP * T))
        total[1] = both_sum.astype(bf16)

        def third(j, carry):
            remote_to(total.at[1], done.at[mine], s_8, r_8, near_peer(j)).start()
            return carry

        lax.fori_loop(1, 16, third, 0)
        pltpu.make_async_copy(total.at[1], done.at[mine], r_8).start()

    xhat = xhat_s[...]
    out = scale_s[:, 0:1] * (
        s - jnp.mean(s, -1, keepdims=True) - xhat * jnp.mean(s * xhat, -1, keepdims=True)
    )
    row = iota((T, T), 0)
    col = iota((T, T), 1)
    unorder = jnp.where(place_of(col) == row, 1.0, 0.0).astype(bf16)
    out_ref[0] = dot(unorder, out.astype(bf16)).astype(bf16)

    drain(done, r_8)
    for p in range(2):
        for c in range(6):
            tile = done[p * 6 + c].astype(f32)
            merged_ref[2 * p, :, 128 * c : 128 * c + 128] = tile[:R]
            merged_ref[2 * p + 1, :, 128 * c : 128 * c + 128] = tile[R:]

    drain(kv.at[pl.ds(0, (SEQ - 1) * FAR)], s_kv)
    drain(qda.at[pl.ds(0, (CHIPS - 1) * FAR)], s_qd)
    drain(recv2.at[pl.ds(0, (CHIPS - 1) * FAR)], s_2)
    drain(recv3.at[pl.ds(0, (CHIPS - 1) * FAR)], s_3)
    drain(rkvg.at[pl.ds(0, (SEQ - 1) * FAR)], s_4)
    drain(rdq.at[pl.ds(0, (CHIPS - 1) * FAR)], s_5)

    @pl.when(mine < SLICES)
    def _():
        drain(one.at[pl.ds(0, SLICES - 1)], s_6)
        drain(two.at[pl.ds(0, 15)], s_7)
        drain(one.at[pl.ds(0, 15)], s_8)

    @pl.when(mine >= SLICES)
    def _():
        drain(one.at[pl.ds(0, SLICES)], s_6)


def shape(*dims, kind=bf16):
    return jax.ShapeDtypeStruct(dims, kind)


def whole():
    return pl.BlockSpec(memory_space=pltpu.VMEM)


def per_device(
    tiles, cotangent, gain, query_matrix, key_matrix, value_matrix, w_out,
    query_down_factor, query_up_factor, value_down_factor, value_up_factor, valid_count,
):
    buf = pltpu.VMEM
    sem = pltpu.SemaphoreType.DMA
    return pl.pallas_call(
        layer_kernel,
        out_shape=[shape(1, T, D), shape(4, R, D, kind=f32)],
        in_specs=[pl.BlockSpec(memory_space=pltpu.SMEM)] + [whole()] * 11,
        out_specs=[whole()] * 2,
        scratch_shapes=[
            buf((T, D), f32), buf((T, 128), f32), buf((T, D), bf16), buf((2 * R, T), f32),
            buf((T, D), bf16), buf((T, D), bf16), buf((T, D), bf16),
            buf((D, T), bf16), buf((D, T), bf16), buf((D, T), bf16), buf((D, T), bf16),
            buf((H, FAR, 128), bf16), buf((H, FAR, 128), bf16),
            buf((H, T, T), bf16), buf((H, 256, PAIR), bf16),
            buf((T, T), bf16), buf((256, PAIR), bf16),
            buf((H, T), f32), buf((D, T), f32), buf((H, T), f32),
            buf((D, T), bf16), buf((T, D), bf16), buf((D, T), f32), buf((D, PAIR), f32),
            buf((T, D), f32), buf((T, D), f32),
            buf((256, D), bf16), buf((256, D), bf16), buf((D, 256), bf16), buf((D, 256), bf16),
            buf((256, D), f32), buf((256, D), f32),
            buf((2, PAIR, D), bf16), buf((2, PAIR, D), bf16),
            buf((T, 128), bf16), buf((256, 128), bf16), buf((256, T), bf16),
            buf((256, 128), f32), buf((256, 128), f32),
            buf((FAR, 128), f32), buf((256, 128), f32),
            buf((T, 128), bf16), buf((256, 128), bf16), buf((T, 128), bf16), buf((256, 128), bf16),
            buf((SLICES, 16, 128), bf16), buf((16, 16, 128), bf16), buf((2, 16, 128), bf16),
            buf((16, 16, 128), bf16), buf((SLICES, 16, 128), bf16),
            sem, sem, sem, sem, sem((4,)), sem((4,)), sem, sem, sem, sem, sem, sem, sem, sem,
            sem, sem, sem, sem, sem, sem, sem, sem,
        ],
        compiler_params=pltpu.CompilerParams(
            vmem_limit_bytes=VMEM_LIMIT, collective_id=0, has_side_effects=True
        ),
        name="layer",
    )(
        valid_count, tiles, cotangent, gain, query_matrix, key_matrix, value_matrix, w_out,
        query_down_factor.T, query_up_factor, value_down_factor.T, value_up_factor,
    )


def solution(mesh):
    placed = (P("dp", "seq", None),) * 2 + (P(),) * 9 + (P("dp"),)
    return jax.shard_map(
        per_device,
        mesh=mesh,
        in_specs=placed,
        out_specs=(P("dp", "seq", None), P()),
        check_vma=False,
    )
```

time: 731 us -> 67.8 us (0.09); the launches traced: 723 us -> 67.6 us
  waiting for transfers between devices: 278 us -> 0 us
  local copies, waits for them, and re-layouts: 141 us -> 2.74 us
  matrix products: 104 us -> 0 us
  other arithmetic: 104 us -> 0 us
  blocking collectives: 76.6 us -> 0 us
  Pallas kernels: 0 us -> 63.6 us
  between operations: 15.4 us -> 1.3 us
    psum x1 -> x0, waiting for transfers between devices: 235 us -> none  [per_device(): merged_low_rank = lax.psum(low_rank_couplets, ('dp', 'seq'))]
    dot_general x37 -> x0, matrix products: 104 us -> none  [the longest x3 18 us: exponentials(): jnp.einsum('...fou,...iou->...ofi', probe_embeddings, address_embeddings,...]
    scatter-add x10 -> x0, other arithmetic: 80.4 us -> none  [the longest x2 18.7 us: per_device(): key_gradient = key_gradient.at[::MIDDLE_DILATION].add(local_couple_keys)....]
    all_gather x2 -> x0, blocking collectives: 76.6 us -> none  [the longest x1 40.9 us: per_device(): lax.all_gather(flattened_keys[::step_stride], 'seq', axis=0, tiled=True)]
    slice x21 -> x0, local copies, waits for them, and re-layouts: 65 us -> none  [the longest x1 10 us: per_device(): couple_queries = probe_embeddings[::MIDDLE_DILATION]]
    pallas_call x0 -> x1, Pallas kernels: none -> 63.6 us  [per_device(): pl.pallas_call(layer_kernel, out_shape=[shape(1, T, D), shape(4, R, D, ki...]
    unnamed x3 -> x0, waiting for transfers between devices: 43.5 us -> none
    scatter-add x5 -> x0, local copies, waits for them, and re-layouts: 13.3 us -> none  [the longest x1 3.47 us: per_device(): mixed_output.at[::step_stride].add(value_mixing(far_probs, all_v))]
  transfers between devices with their start and end apart: 6 -> 0, of which waited for: 2 -> 0; matrix products, arithmetic and copies ran while one was open for 28% -> 0% of each run, Pallas kernels for 0% -> 0%
where the time goes in v1:
time: 67.8 us; the launch traced here: 67.6 us
  Pallas kernels  63.6 us (94%)
  local copies, waits for them, and re-layouts  2.74 us (4%)
  between operations  1.3 us (2%)
    pallas_call x1, Pallas kernels, per_device(): pl.pallas_call(layer_kernel, out_shape=[shape(1, T, D), shape(4, R, D, ki...  63.6 us
    unnamed x4, local copies, waits for them, and re-layouts  2.74 us

profile of v1, /device:TPU:1, one launch (start us, length us, event | category | flops | bytes accessed | tf_op | source)
XLA Modules:
  0.0 67.6 jit_solution(10264308077745130304)
XLA Ops:
  1.3 63.6 %layer.1 = (bf16[1,512,768]{2,1,0:T(8,128)(2,1)}, f32[4,8,768]{2,1,0:T(8,128)}) custom-call(s32[1]{0:T(128)S(6)} %copy.16.valid_ref, bf16[1,512,768]{2,1,0:T(8,128)(2,1)} %tiles_ref.1, bf16[1,512,768]{2,1,0:T(8,128)(2,1)} %cot_ref.1, bf16[768]{0:T(1024)(128)(2,1)} %gain_ref.1, bf16[768,768]{1,0:T(8,128)(2,1)} %wq_ref.1, bf16[768,768]{1,0:T(8,128)(2,1)} %wk_ref.1, ...), custom_call_target="tpu_custom_call" | custom-call | tf_op jit(solution)/shard_map/layer/pallas_call | solution.py:555
  64.9 0.0 copy-start
  64.9 2.1 %copy.17 = bf16[1,512,768]{2,1,0:T(8,128)(2,1)} copy(bf16[1,512,768]{2,1,0:T(8,128)(2,1)} %get-tuple-element.4) | data formatting | bytes 1572864
  67.0 0.0 copy-done
  67.0 0.6 copy.18
Async XLA Ops:
  64.9 2.1 %copy-start = (f32[4,8,768]{2,1,0:T(8,128)S(1)}, f32[4,8,768]{2,1,0:T(8,128)}, u32[]{:S(2)}) copy-start(f32[4,8,768]{2,1,0:T(8,128)} %get-tuple-element.5) | copy-start | bytes 294916

commit v2 on v1

v2 whole, which is shorter than its diff:
```python
import math

import jax
import jax.numpy as jnp
from jax import lax
from jax.experimental import pallas as pl
from jax.experimental.pallas import tpu as pltpu
from jax.sharding import PartitionSpec as P

T = 512
D = 768
H = 16
W = 48
R = 8
PAIR = 128
FAR = 16
SEQ = 32
DP = 8
CHIPS = 16
GROUPS = 2
SLICES = 12
PER = 8
EPS = 1e-5
LOG2E = math.log2(math.e)
SHARP = 1.0 / math.sqrt(W)
LN2 = math.log(2.0)
MESH = pl.DeviceIdType.MESH
f32 = jnp.float32
bf16 = jnp.bfloat16
VMEM_LIMIT = 56 * 1024 * 1024


def iota(shape, axis):
    return lax.broadcasted_iota(jnp.int32, shape, axis)


def dot(a, b):
    return jnp.dot(a, b, preferred_element_type=f32)


def dot_nt(a, b):
    return lax.dot_general(a, b, (((1,), (1,)), ((), ())), preferred_element_type=f32)


def place_of(row):
    return (row & 15) * 32 + ((row >> 4) & 7) * 4 + (row >> 7)


def order_matrix():
    place = place_of(iota((T, 128), 0))
    lane = iota((T, 128), 1)
    parts = [jnp.where(place == lane + 128 * c, 1.0, 0.0) for c in range(4)]
    return jnp.concatenate(parts, 1).astype(bf16)


def halves(value):
    upper = value.astype(bf16)
    lower = (value - upper.astype(f32)).astype(bf16)
    return upper, lower


def normalize(x):
    center = x - jnp.mean(x, -1, keepdims=True)
    inverse = lax.rsqrt(jnp.mean(center * center, -1, keepdims=True) + EPS)
    return center * inverse, inverse


def window(hh):
    low = W * hh
    first = low // 128
    last = (low + W - 1) // 128
    return first * 128, (last - first + 1) * 128, low - first * 128


def pair_window(p):
    low = 2 * W * p
    first = low // 128
    last = (low + 2 * W - 1) // 128
    return first * 128, (last - first + 1) * 128, low - first * 128


def lane_mask(width, off):
    lane = iota((1, width), 1)
    return jnp.where((lane >= off) & (lane < off + W), 1.0, 0.0).astype(bf16)


def pad_rows(block, off, width):
    parts = []
    if off:
        parts.append(jnp.zeros((off, block.shape[1]), block.dtype))
    parts.append(block)
    rest = width - off - block.shape[0]
    if rest:
        parts.append(jnp.zeros((rest, block.shape[1]), block.dtype))
    return jnp.concatenate(parts, 0)


def down_rows(qd_ref, vd_ref):
    return jnp.concatenate(
        [qd_ref[...].astype(f32), vd_ref[...].astype(f32), jnp.zeros((112, D), f32)], 0
    ).astype(bf16)


def up_padded(u_ref, at):
    return pad_rows(u_ref[...].astype(f32), at, 128).astype(bf16)


def layer_kernel(
    valid_ref, tiles_ref, cot_hbm, gain_ref, wq_hbm, wk_hbm, wv_hbm, wo_hbm,
    qd_ref, qu_ref, vd_ref, vu_ref,
    out_ref, done,
    cot_ref, wq_ref, wk_ref, wv_ref, wo_ref, s_in,
    xhat_s, scale_s, normed_s, lift_s, q_ref, k_ref, v_ref, qt_ref, kt_ref, vt_ref, dat_ref,
    sfar,
    e0, e1, mask0, mask1, tot, mix, dlt, dapt, dap, dqt, dq1t, dk, dv,
    k1, v1, k1t, v1t, dk1, dv1, gsend, gback,
    same, other, kv, qda, fe, send2, recv2, send3, recv3, bsame, bother, rsame, rother,
    part, one, total, two,
    s_kv, r_kv, s_qd, r_qd, s_pair, r_pair, s_2, r_2, s_3, r_3, s_4, r_4, s_5, r_5, s_g, r_g,
    s_6, r_6, s_7, r_7, s_8, r_8,
):
    dp = lax.axis_index("dp")
    me = lax.axis_index("seq")
    chip = lax.div(me, 2)
    core = lax.rem(me, 2)
    mate = chip * 2 + (1 - core)
    mine = lax.rem(me, 16)
    half = lax.div(me, 16)
    plane = dp * 2 + half
    valid = valid_ref[0]

    def near_peer(j):
        return {"seq": half * 16 + lax.rem(mine + j, 16)}

    def across_peer(j):
        other = lax.rem(plane + j, 16)
        return {"dp": lax.div(other, 2), "seq": lax.rem(other, 2) * 16 + mine}

    barrier = pltpu.get_barrier_semaphore()

    for j in range(1, SEQ):
        pl.semaphore_signal(
            barrier, inc=1, device_id={"seq": lax.rem(me + j, SEQ)}, device_id_type=MESH
        )
    for j in range(1, 16):
        pl.semaphore_signal(barrier, inc=1, device_id=across_peer(j), device_id_type=MESH)

    def remote_to(src, dst, send, recv, peer):
        return pltpu.make_async_remote_copy(
            src_ref=src, dst_ref=dst, send_sem=send, recv_sem=recv,
            device_id=peer, device_id_type=MESH,
        )

    def remote(src, dst, send, recv, peer):
        return remote_to(src, dst, send, recv, {"seq": peer})

    def drain(ref, sem):
        pltpu.make_async_copy(ref, ref, sem).wait()

    loads = [
        pltpu.make_async_copy(src, dst, s_in.at[i])
        for i, (src, dst) in enumerate(
            [(wq_hbm, wq_ref), (wk_hbm, wk_ref), (wv_hbm, wv_ref), (cot_hbm, cot_ref), (wo_hbm, wo_ref)]
        )
    ]
    for load in loads:
        load.start()

    order = order_matrix()
    x = dot(order, tiles_ref[0])
    xhat, inverse_dev = normalize(x)
    xhat_s[...] = xhat
    scale_s[...] = jnp.broadcast_to(inverse_dev, (T, 128))
    normed = (xhat * gain_ref[...].astype(f32)).astype(bf16)
    normed_s[...] = normed
    down = down_rows(qd_ref, vd_ref)
    uq = up_padded(qu_ref, 0)
    uv = up_padded(vu_ref, R)
    lift = dot_nt(normed, down)
    both = jnp.concatenate(halves(lift), 1)
    lift_s[...] = lift.T[: 2 * R]
    loads[0].wait()
    q = dot(normed, wq_ref[...]) + 2.0 * dot(both, jnp.concatenate([uq, uq], 0))
    q = (q * (SHARP * LOG2E)).astype(bf16)
    q_ref[...] = q
    qt_ref[...] = q.T
    loads[1].wait()
    k = dot(normed, wk_ref[...]).astype(bf16)
    k_ref[...] = k
    kt_ref[...] = k.T
    loads[2].wait()
    v = (dot(normed, wv_ref[...]) + 2.0 * dot(both, jnp.concatenate([uv, uv], 0))).astype(bf16)
    v_ref[...] = v
    vt_ref[...] = v.T
    loads[3].wait()
    loads[4].wait()
    cot = dot(order, cot_ref[0]).astype(bf16)
    da = dot_nt(cot, wo_ref[...]).astype(bf16)
    dat_ref[...] = da.T
    gap = jnp.zeros((FAR, 64 - W), f32)
    qf, kf, vf, df = (rows[:FAR].astype(f32) for rows in (q, k, v, da))
    for h in range(H):
        cut = slice(W * h, W * h + W)
        four = [kf[:, cut], gap, vf[:, cut], gap, qf[:, cut], gap, df[:, cut], gap]
        sfar[h] = jnp.concatenate(four, 1).astype(bf16)

    pl.semaphore_wait(barrier, SEQ - 1 + 15)

    def slot(c):
        return pl.ds(pl.multiple_of(c * FAR, FAR), FAR)

    def around(j):
        return lax.rem(chip + j, CHIPS)

    for j in range(CHIPS):
        there = around(j)
        if j:
            remote(sfar.at[there], same.at[slot(chip)], s_kv, r_kv, there * 2 + core).start()
        keys_only = sfar.at[there, :, pl.ds(0, 128)]
        remote(keys_only, other.at[slot(chip)], s_qd, r_qd, there * 2 + (1 - core)).start()
    pltpu.make_async_copy(sfar.at[chip], same.at[slot(chip)], r_kv).start()

    near = pl.ds(0, PAIR)
    pair_copies = [
        remote(k_ref.at[near], k1, s_pair.at[0], r_pair.at[0], mate),
        remote(v_ref.at[near], v1, s_pair.at[1], r_pair.at[1], mate),
        remote(kt_ref.at[:, near], k1t, s_pair.at[2], r_pair.at[2], mate),
        remote(vt_ref.at[:, near], v1t, s_pair.at[3], r_pair.at[3], mate),
    ]
    for copy in pair_copies:
        copy.start()

    row = iota((T, 128), 0)
    col = iota((T, 128), 1)
    seen = me * T + place_of(row) < valid
    for c in range(4):
        open0 = seen | (row == col + 128 * c)
        mask0[:, 128 * c : 128 * c + 128] = jnp.where(open0, jnp.inf, 0.0).astype(bf16)
    row = iota((PAIR, 2 * PAIR), 0)
    mask1[...] = jnp.where(mate * T + place_of(row) < valid, jnp.inf, 0.0).astype(bf16)
    dk[...] = jnp.zeros_like(dk)
    dv[...] = jnp.zeros_like(dv)
    dk1[...] = jnp.zeros_like(dk1)
    dv1[...] = jnp.zeros_like(dv1)

    def place(g, hh):
        base, width, off = window(hh)
        lanes = pl.ds(pl.multiple_of(g * 384 + base, 128), width)
        rows = pl.ds(pl.multiple_of(g * 384 + W * hh, 16), W)
        return lanes, rows, width, off

    def eight(g):
        return pl.ds(pl.multiple_of(g * PER, PER), PER)

    def forward0(g):
        totals = []
        for hh in range(PER):
            lanes, rows, width, off = place(g, hh)
            ask = pad_rows(qt_ref[rows, :], off, width)
            expo = jnp.exp2(dot(k_ref[:, lanes], ask)).astype(bf16)
            expo = jnp.minimum(expo, mask0[...])
            corner = expo[:PAIR, :PAIR]
            upper = jnp.concatenate([corner + corner, expo[:PAIR, PAIR:]], 1)
            expo = jnp.concatenate([upper, expo[PAIR:]], 0)
            e0[g * PER + hh] = expo
            value = jnp.concatenate([vt_ref[rows, :], jnp.ones((16, T), bf16)], 0)
            mixed = dot(value, expo)
            totals.append(mixed[W : W + 1])
            mix[rows, :] = mixed[:W]
        tot[eight(g), :] = jnp.concatenate(totals, 0)

    def pair_place(g, p):
        base, width, off = pair_window(p)
        lanes = pl.ds(pl.multiple_of(g * 384 + base, 128), width)
        low = pl.ds(pl.multiple_of(g * 384 + 2 * W * p, 16), W)
        high = pl.ds(pl.multiple_of(g * 384 + 2 * W * p + W, 16), W)
        both = pl.ds(pl.multiple_of(g * 384 + 2 * W * p, 16), 2 * W)
        return lanes, low, high, both, width, off

    def side_by_side(low, high, off, width):
        none = jnp.zeros((W, PAIR), bf16)
        block = jnp.concatenate(
            [jnp.concatenate([low, none], 1), jnp.concatenate([none, high], 1)], 0
        )
        return pad_rows(block, off, width)

    def stacked(rows, off, width):
        return jnp.concatenate([rows * lane_mask(width, off), rows * lane_mask(width, off + W)], 0)

    def forward1(g):
        totals = []
        for p in range(PER // 2):
            lanes, low, high, both, width, off = pair_place(g, p)
            ask = side_by_side(qt_ref[low, near], qt_ref[high, near], off, width)
            expo = jnp.exp2(dot(k1[:, lanes], ask)).astype(bf16)
            expo = jnp.minimum(expo, mask1[...])
            e1[g * (PER // 2) + p] = expo
            value = jnp.concatenate([v1t[both, :], jnp.ones((16, PAIR), bf16)], 0)
            mixed = dot(value, expo)
            mix[low, near] += mixed[:W, :PAIR]
            mix[high, near] += mixed[W : 2 * W, PAIR:]
            totals.append(mixed[2 * W : 2 * W + 1, :PAIR])
            totals.append(mixed[2 * W : 2 * W + 1, PAIR:])
        tot[eight(g), near] += jnp.concatenate(totals, 0)

    for g in range(1):
        forward0(g)

    drain(same, r_kv)
    drain(other, r_qd)
    kv[pl.ds(0, 256)] = same[:, :128]
    kv[pl.ds(256, 256)] = other[...]
    qda[...] = same[:, 128:]
    lane = iota((1, 128), 1)
    low = jnp.where(lane < 64, 1.0, 0.0).astype(bf16)
    high = jnp.where(lane >= 64, 1.0, 0.0).astype(bf16)
    i2 = iota((256, T), 0)
    j2 = iota((1, T), 1)
    j2_core = (j2 >> 8) * (1 - core) + (1 - (j2 >> 8)) * core
    j2_pos = (((j2 & 255) >> 4) * 2 + j2_core) * T + (j2 & 15) * 32
    open2 = (j2_pos < valid) | (j2 == i2)
    far_expo = jnp.exp2(dot_nt(qda[...], kv[...] * low))
    far_expo = jnp.where(open2, far_expo, 0.0).astype(bf16)
    fe[...] = far_expo
    first_lane = jnp.where(lane == 0, 1.0, 0.0).astype(bf16)
    far_mixed = dot(far_expo, kv[...] * high + first_lane)
    far_r = jnp.sum(
        jnp.where(lane >= 64, qda[...].astype(f32) * far_mixed, 0.0), 1, keepdims=True
    )
    far_t = far_mixed[:, 0:1]
    send2[...] = jnp.where(lane == chip, far_t, 0.0) + jnp.where(lane == 64 + chip, far_r, 0.0)

    for j in range(1, CHIPS):
        there = around(j)
        remote(send2.at[slot(there)], recv2.at[slot(chip)], s_2, r_2, there * 2 + core).start()
    pltpu.make_async_copy(send2.at[slot(chip)], recv2.at[slot(chip)], r_2).start()

    forward0(1)
    for copy in pair_copies:
        copy.wait()
    for g in range(GROUPS):
        forward1(g)

    drain(recv2, r_2)
    gathered = recv2[pl.ds(0, FAR)]
    for c in range(1, CHIPS):
        gathered = gathered + recv2[pl.ds(c * FAR, FAR)]
    turned = jnp.concatenate([gathered, jnp.zeros((PAIR - FAR, 128), f32)], 0).T
    tot[:, near] += turned[:H]
    inverse = 1.0 / tot[...]
    tot[...] = inverse
    far_sums = jnp.concatenate([turned[64 : 64 + H], jnp.zeros((H, T - PAIR), f32)], 1)
    dlt[...] = far_sums * inverse * inverse
    for h in range(H):
        rows = pl.ds(W * h, W)
        this = tot[h : h + 1, :]
        scaled = (dat_ref[rows, :].astype(f32) * this).astype(bf16)
        dapt[rows, :] = scaled
        own = jnp.sum(scaled.astype(f32) * mix[rows, :], 0, keepdims=True)
        dlt[h : h + 1, :] += own * this
    filler = jnp.zeros((64 - H, 128), f32)
    send3[...] = jnp.concatenate([tot[:, near], filler, dlt[:, near], filler], 0).T[:FAR]

    for j in range(1, CHIPS):
        there = around(j)
        remote(send3, recv3.at[slot(chip)], s_3, r_3, there * 2 + core).start()
    pltpu.make_async_copy(send3, recv3.at[slot(chip)], r_3).start()
    dap[...] = dapt[...].T

    def backward0(g):
        deltas = dlt[eight(g), :]
        for hh in range(PER):
            lanes, rows, width, off = place(g, hh)
            expo = e0[g * PER + hh]
            dprob = dot(v_ref[:, lanes], pad_rows(dapt[rows, :], off, width))
            dscore = expo * (dprob - deltas[hh : hh + 1]).astype(bf16)
            e0[g * PER + hh] = dscore
            dqt[rows, :] = dot(kt_ref[rows, :], dscore)
            dv[:, lanes] += dot(expo, dap[:, lanes] * lane_mask(width, off))

    def backward1(g):
        deltas = dlt[eight(g), near]
        for p in range(PER // 2):
            lanes, low, high, both, width, off = pair_place(g, p)
            expo = e1[g * (PER // 2) + p]
            dprob = dot(v1[:, lanes], side_by_side(dapt[low, near], dapt[high, near], off, width))
            delta = jnp.concatenate([deltas[2 * p : 2 * p + 1], deltas[2 * p + 1 : 2 * p + 2]], 1)
            dscore = expo * (dprob - delta).astype(bf16)
            dq = dot(k1t[both, :], dscore)
            dq1t[low, :] = dq[:W, :PAIR]
            dq1t[high, :] = dq[W:, PAIR:]
            dv1[:, lanes] += dot(expo, stacked(dap[near, lanes], off, width))
            dk1[:, lanes] += dot(dscore, stacked(q_ref[near, lanes], off, width))

    def keys0(g):
        for hh in range(PER):
            lanes, rows, width, off = place(g, hh)
            dk[:, lanes] += dot(e0[g * PER + hh], q_ref[:, lanes] * lane_mask(width, off))

    for g in range(GROUPS):
        backward1(g)
    gsend[0] = dk1[...].astype(bf16)
    gsend[1] = dv1[...].astype(bf16)
    grad_copy = remote(gsend, gback, s_g, r_g, mate)
    grad_copy.start()
    backward0(0)

    drain(recv3, r_3)
    scales = recv3[...]
    far_inv = jnp.sum(jnp.where(lane == chip, scales, 0.0), 1, keepdims=True)
    far_del = jnp.sum(jnp.where(lane == 64 + chip, scales, 0.0), 1, keepdims=True)
    far_grads = jnp.where(lane >= 64, qda[...].astype(f32) * far_inv, 0.0).astype(bf16)
    far_back = fe[...].astype(f32)
    far_ds = far_back * (dot_nt(far_grads, kv[...] * high) - far_del)
    back_kv = (
        dot(far_ds.T.astype(bf16), qda[...] * low) + dot(far_back.T.astype(bf16), far_grads)
    ).astype(bf16)
    bsame[:, :128] = back_kv[:256]
    bsame[:, 128:] = dot(far_ds.astype(bf16), kv[...] * low).astype(bf16)
    bother[...] = back_kv[256:]
    for j in range(CHIPS):
        there = around(j)
        if j:
            remote(
                bsame.at[slot(there)], rsame.at[slot(chip)], s_4, r_4, there * 2 + core
            ).start()
        remote(
            bother.at[slot(there)], rother.at[slot(chip)], s_5, r_5, there * 2 + (1 - core)
        ).start()
    pltpu.make_async_copy(bsame.at[slot(chip)], rsame.at[slot(chip)], r_4).start()

    backward0(1)

    grad_copy.wait()
    drain(rsame, r_4)
    drain(rother, r_5)
    keys_back, values_back, asks_back = [], [], []
    for h in range(H):
        both_back = rsame[pl.ds(h * FAR, FAR)].astype(f32)
        here = both_back[:, :128] + rother[pl.ds(h * FAR, FAR)].astype(f32)
        keys_back.append(here[:, :W])
        values_back.append(here[:, 64 : 64 + W])
        asks_back.append(both_back[:, 128 : 128 + W])
    few = pl.ds(0, FAR)
    dv[near] += gback[1].astype(f32)
    dv[few] += jnp.concatenate(values_back, 1)
    dk[near] = gback[0].astype(f32)
    dk[few] += jnp.concatenate(keys_back, 1)
    dqt[:, near] += dq1t[...]
    gq = dqt[...].T
    gq = jnp.concatenate([gq[:FAR] + jnp.concatenate(asks_back, 1), gq[FAR:]], 0)
    gq = (gq * SHARP).astype(bf16)
    gv = dv[...].astype(bf16)
    back = dot_nt(gq, uq) + dot_nt(gv, uv)
    back_both = jnp.concatenate(halves(back), 1)
    bu, bl = halves(back.T[: 2 * R])
    lu, ll = halves(lift_s[...])
    from_back = dot(jnp.concatenate([bu, bl], 0), normed_s[...])
    from_back = 2.0 * (from_back[:16] + from_back[16:])
    lifts = jnp.concatenate([lu, ll], 0)
    from_q = dot(lifts, gq)
    from_q = 2.0 * (from_q[:R] + from_q[16 : 16 + R])
    from_v = dot(lifts, gv)
    from_v = 2.0 * (from_v[R:16] + from_v[16 + R : 32])
    pairs = [
        jnp.concatenate([from_back[:R], from_q], 0), jnp.concatenate([from_back[R:16], from_v], 0)
    ]
    for p in range(2):
        for c in range(6):
            part[p * 6 + c] = pairs[p][:, 128 * c : 128 * c + 128].astype(bf16)

    def first(j, carry):
        there = lax.rem(mine + j, 16)

        @pl.when(there < SLICES)
        def _():
            remote_to(part.at[there], one.at[mine], s_6, r_6, near_peer(j)).start()

        return carry

    lax.fori_loop(1, 16, first, 0)

    @pl.when(mine < SLICES)
    def _():
        pltpu.make_async_copy(part.at[mine], one.at[mine], r_6).start()

    for g in range(GROUPS):
        keys0(g)

    @pl.when(mine < SLICES)
    def _():
        drain(one, r_6)
        total[0] = jnp.sum(one[...].astype(f32), 0).astype(bf16)

        for j in range(1, 16):
            remote_to(total.at[0], two.at[plane], s_7, r_7, across_peer(j)).start()
        pltpu.make_async_copy(total.at[0], two.at[plane], r_7).start()

    gk = (dk[...] * LN2).astype(bf16)
    grad = (
        dot_nt(gq, wq_ref[...])
        + dot_nt(gk, wk_ref[...])
        + dot_nt(gv, wv_ref[...])
        + 2.0 * dot(back_both, jnp.concatenate([down, down], 0))
    )
    s = grad * gain_ref[...].astype(f32)

    @pl.when(mine < SLICES)
    def _():
        drain(two, r_7)
        both_sum = jnp.sum(two[...].astype(f32), 0) * (1.0 / math.sqrt(SEQ * DP * T))
        total[1] = both_sum.astype(bf16)

        for j in range(1, 16):
            remote_to(total.at[1], done.at[mine], s_8, r_8, near_peer(j)).start()
        pltpu.make_async_copy(total.at[1], done.at[mine], r_8).start()

    xhat = xhat_s[...]
    out = scale_s[:, 0:1] * (
        s - jnp.mean(s, -1, keepdims=True) - xhat * jnp.mean(s * xhat, -1, keepdims=True)
    )
    out_ref[...] = out.astype(bf16)
    drain(done, r_8)

    drain(same.at[pl.ds(0, (CHIPS - 1) * FAR)], s_kv)
    drain(other, s_qd)
    drain(recv2.at[pl.ds(0, (CHIPS - 1) * FAR)], s_2)
    drain(recv3.at[pl.ds(0, (CHIPS - 1) * FAR)], s_3)
    drain(rsame.at[pl.ds(0, (CHIPS - 1) * FAR)], s_4)
    drain(rother, s_5)

    @pl.when(mine < SLICES)
    def _():
        drain(one.at[pl.ds(0, SLICES - 1)], s_6)
        drain(two.at[pl.ds(0, 15)], s_7)
        drain(one.at[pl.ds(0, 15)], s_8)

    @pl.when(mine >= SLICES)
    def _():
        drain(one.at[pl.ds(0, SLICES)], s_6)


def place_kernel(y_ref, done_ref, out_ref, merged_ref):
    unorder = jnp.where(place_of(iota((1, T), 1)) == iota((T, T), 0), 1.0, 0.0).astype(bf16)
    out_ref[0] = dot(unorder, y_ref[...]).astype(bf16)
    for p in range(2):
        for c in range(6):
            tile = done_ref[p * 6 + c].astype(f32)
            merged_ref[2 * p, :, 128 * c : 128 * c + 128] = tile[:R]
            merged_ref[2 * p + 1, :, 128 * c : 128 * c + 128] = tile[R:]


def shape(*dims, kind=bf16):
    return jax.ShapeDtypeStruct(dims, kind)


def whole():
    return pl.BlockSpec(memory_space=pltpu.VMEM)


def far():
    return pl.BlockSpec(memory_space=pl.ANY)


def per_device(
    tiles, cotangent, gain, query_matrix, key_matrix, value_matrix, w_out,
    query_down_factor, query_up_factor, value_down_factor, value_up_factor, valid_count,
):
    buf = pltpu.VMEM
    sem = pltpu.SemaphoreType.DMA
    y, done = pl.pallas_call(
        layer_kernel,
        out_shape=[shape(T, D), shape(SLICES, 16, 128)],
        in_specs=[pl.BlockSpec(memory_space=pltpu.SMEM), whole(), far(), whole()] + [far()] * 4
        + [whole()] * 4,
        out_specs=[whole()] * 2,
        scratch_shapes=[
            buf((1, T, D), bf16), buf((D, D), bf16), buf((D, D), bf16), buf((D, D), bf16),
            buf((D, D), bf16), sem((5,)),
            buf((T, D), f32), buf((T, 128), f32), buf((T, D), bf16), buf((2 * R, T), f32),
            buf((T, D), bf16), buf((T, D), bf16), buf((T, D), bf16),
            buf((D, T), bf16), buf((D, T), bf16), buf((D, T), bf16), buf((D, T), bf16),
            buf((H, FAR, 256), bf16),
            buf((H, T, T), bf16), buf((H // 2, PAIR, 256), bf16),
            buf((T, T), bf16), buf((PAIR, 256), bf16),
            buf((H, T), f32), buf((D, T), f32), buf((H, T), f32),
            buf((D, T), bf16), buf((T, D), bf16), buf((D, T), f32), buf((D, PAIR), f32),
            buf((T, D), f32), buf((T, D), f32),
            buf((PAIR, D), bf16), buf((PAIR, D), bf16), buf((D, PAIR), bf16), buf((D, PAIR), bf16),
            buf((PAIR, D), f32), buf((PAIR, D), f32),
            buf((2, PAIR, D), bf16), buf((2, PAIR, D), bf16),
            buf((256, 256), bf16), buf((256, 128), bf16),
            buf((T, 128), bf16), buf((256, 128), bf16), buf((256, T), bf16),
            buf((256, 128), f32), buf((256, 128), f32),
            buf((FAR, 128), f32), buf((256, 128), f32),
            buf((256, 256), bf16), buf((256, 128), bf16),
            buf((256, 256), bf16), buf((256, 128), bf16),
            buf((SLICES, 16, 128), bf16), buf((16, 16, 128), bf16), buf((2, 16, 128), bf16),
            buf((16, 16, 128), bf16),
            sem, sem, sem, sem, sem((4,)), sem((4,)), sem, sem, sem, sem, sem, sem, sem, sem,
            sem, sem, sem, sem, sem, sem, sem, sem,
        ],
        compiler_params=pltpu.CompilerParams(
            vmem_limit_bytes=VMEM_LIMIT, collective_id=0, has_side_effects=True
        ),
        name="layer",
    )(
        valid_count, tiles, cotangent, gain, query_matrix, key_matrix, value_matrix, w_out,
        query_down_factor.T, query_up_factor, value_down_factor.T, value_up_factor,
    )
    return pl.pallas_call(
        place_kernel,
        out_shape=[shape(1, T, D), shape(4, R, D, kind=f32)],
        in_specs=[whole()] * 2,
        out_specs=[whole()] * 2,
        name="place",
    )(y, done)


def solution(mesh):
    placed = (P("dp", "seq", None),) * 2 + (P(),) * 9 + (P("dp"),)
    return jax.shard_map(
        per_device,
        mesh=mesh,
        in_specs=placed,
        out_specs=(P("dp", "seq", None), P()),
        check_vma=False,
    )
```

time: 67.8 us -> 66.2 us (0.976)
  local copies, waits for them, and re-layouts: 2.74 us -> 0 us
  Pallas kernels: 63.6 us -> 64.7 us
    unnamed x4 -> x0, local copies, waits for them, and re-layouts: 2.74 us -> none
    pallas_call x1 -> x2, Pallas kernels: 63.6 us -> 64.7 us  [the longest x1 62.2 us: per_device(): pl.pallas_call(layer_kernel, out_shape=[shape(T, D), shape(SLICES, 16, 12...]
where the time goes in v2:
time: 66.2 us; the launch traced here: 66 us
  Pallas kernels  64.7 us (98%)
  between operations  1.29 us (2%)
    pallas_call x1, Pallas kernels, per_device(): pl.pallas_call(layer_kernel, out_shape=[shape(T, D), shape(SLICES, 16, 12...  62.2 us
    pallas_call x1, Pallas kernels, per_device(): pl.pallas_call(place_kernel, out_shape=[shape(1, T, D), shape(4, R, D, ki...  2.59 us

profile of v2, /device:TPU:1, one launch (start us, length us, event | category | flops | bytes accessed | tf_op | source)
XLA Modules:
  0.0 66.0 jit_solution(13361113346422448129)
XLA Ops:
  1.3 62.2 %layer.1 = (bf16[512,768]{1,0:T(8,128)(2,1)}, bf16[12,16,128]{2,1,0:T(8,128)(2,1)}) custom-call(s32[1]{0:T(128)S(6)} %copy.14.valid_ref, bf16[1,512,768]{2,1,0:T(8,128)(2,1)} %tiles_ref.1, bf16[1,512,768]{2,1,0:T(8,128)(2,1)} %cot_hbm.1, bf16[768]{0:T(1024)(128)(2,1)} %gain_ref.1, bf16[768,768]{1,0:T(8,128)(2,1)} %wq_hbm.1, bf16[768,768]{1,0:T(8,128)(2,1)} %wk_hbm.1, ...), custom_call_target="tpu_custom_call" | custom-call | tf_op jit(solution)/shard_map/layer/pallas_call | solution.py:571
  63.4 2.6 %place.1 = (bf16[1,512,768]{2,1,0:T(8,128)(2,1)}, f32[4,8,768]{2,1,0:T(8,128)}) custom-call(bf16[512,768]{1,0:T(8,128)(2,1)} %get-tuple-element.4.y_ref, bf16[12,16,128]{2,1,0:T(8,128)(2,1)} %get-tuple-element.5.done_ref), custom_call_target="tpu_custom_call" | custom-call | tf_op jit(solution)/shard_map/place/pallas_call | solution.py:611

commit v3 on v2

--- a/solution.py
+++ b/solution.py
@@ -108,14 +108,14 @@
 def layer_kernel(
     valid_ref, tiles_ref, cot_hbm, gain_ref, wq_hbm, wk_hbm, wv_hbm, wo_hbm,
     qd_ref, qu_ref, vd_ref, vu_ref,
-    out_ref, done,
-    cot_ref, wq_ref, wk_ref, wv_ref, wo_ref, s_in,
-    xhat_s, scale_s, normed_s, lift_s, q_ref, k_ref, v_ref, qt_ref, kt_ref, vt_ref, dat_ref,
+    out_ref, merged_ref,
+    cot_ref, wq_ref, wk_ref, wv_ref, wo_ref, s_in, out_s, s_out,
+    xhat_s, scale_s, normed_s, lift_s, q_ref, k_ref, v_ref, qt_ref, kt_ref, dat_ref,
     sfar,
-    e0, e1, mask0, mask1, tot, mix, dlt, dapt, dap, dqt, dq1t, dk, dv,
-    k1, v1, k1t, v1t, dk1, dv1, gsend, gback,
+    e0, p0, e1, p1, mask0, mask1, tot, rsum, dlt, dap, dqt, dq1t, dk, dv,
+    k1, v1, k1t, dk1, dv1, gsend, gback,
     same, other, kv, qda, fe, send2, recv2, send3, recv3, bsame, bother, rsame, rother,
-    part, one, total, two,
+    part, one, total, two, done,
     s_kv, r_kv, s_qd, r_qd, s_pair, r_pair, s_2, r_2, s_3, r_3, s_4, r_4, s_5, r_5, s_g, r_g,
     s_6, r_6, s_7, r_7, s_8, r_8,
 ):
@@ -124,17 +124,17 @@
     chip = lax.div(me, 2)
     core = lax.rem(me, 2)
     mate = chip * 2 + (1 - core)
-    mine = lax.rem(me, 16)
+    column = lax.rem(me, 16)
     half = lax.div(me, 16)
-    plane = dp * 2 + half
+    mine = dp * 2 + half
     valid = valid_ref[0]
 
-    def near_peer(j):
-        return {"seq": half * 16 + lax.rem(mine + j, 16)}
-
-    def across_peer(j):
-        other = lax.rem(plane + j, 16)
-        return {"dp": lax.div(other, 2), "seq": lax.rem(other, 2) * 16 + mine}
+    def plane_peer(j):
+        there = lax.rem(mine + j, 16)
+        return {"dp": lax.div(there, 2), "seq": lax.rem(there, 2) * 16 + column}
+
+    def column_peer(j):
+        return {"seq": half * 16 + lax.rem(column + j, 16)}
 
     barrier = pltpu.get_barrier_semaphore()
 
@@ -143,7 +143,7 @@
             barrier, inc=1, device_id={"seq": lax.rem(me + j, SEQ)}, device_id_type=MESH
         )
     for j in range(1, 16):
-        pl.semaphore_signal(barrier, inc=1, device_id=across_peer(j), device_id_type=MESH)
+        pl.semaphore_signal(barrier, inc=1, device_id=plane_peer(j), device_id_type=MESH)
 
     def remote_to(src, dst, send, recv, peer):
         return pltpu.make_async_remote_copy(
@@ -160,7 +160,7 @@
     loads = [
         pltpu.make_async_copy(src, dst, s_in.at[i])
         for i, (src, dst) in enumerate(
-            [(wq_hbm, wq_ref), (wk_hbm, wk_ref), (wv_hbm, wv_ref), (cot_hbm, cot_ref), (wo_hbm, wo_ref)]
+            [(cot_hbm, cot_ref), (wo_hbm, wo_ref), (wq_hbm, wq_ref), (wk_hbm, wk_ref), (wv_hbm, wv_ref)]
         )
     ]
     for load in loads:
@@ -168,6 +168,11 @@
 
     order = order_matrix()
     x = dot(order, tiles_ref[0])
+    loads[0].wait()
+    loads[1].wait()
+    cot = dot(order, cot_ref[0]).astype(bf16)
+    da = dot_nt(cot, wo_ref[...]).astype(bf16)
+    dat_ref[...] = da.T
     xhat, inverse_dev = normalize(x)
     xhat_s[...] = xhat
     scale_s[...] = jnp.broadcast_to(inverse_dev, (T, 128))
@@ -179,24 +184,18 @@
     lift = dot_nt(normed, down)
     both = jnp.concatenate(halves(lift), 1)
     lift_s[...] = lift.T[: 2 * R]
-    loads[0].wait()
+    loads[2].wait()
+    loads[3].wait()
+    loads[4].wait()
     q = dot(normed, wq_ref[...]) + 2.0 * dot(both, jnp.concatenate([uq, uq], 0))
     q = (q * (SHARP * LOG2E)).astype(bf16)
     q_ref[...] = q
     qt_ref[...] = q.T
-    loads[1].wait()
     k = dot(normed, wk_ref[...]).astype(bf16)
     k_ref[...] = k
     kt_ref[...] = k.T
-    loads[2].wait()
     v = (dot(normed, wv_ref[...]) + 2.0 * dot(both, jnp.concatenate([uv, uv], 0))).astype(bf16)
     v_ref[...] = v
-    vt_ref[...] = v.T
-    loads[3].wait()
-    loads[4].wait()
-    cot = dot(order, cot_ref[0]).astype(bf16)
-    da = dot_nt(cot, wo_ref[...]).astype(bf16)
-    dat_ref[...] = da.T
     gap = jnp.zeros((FAR, 64 - W), f32)
     qf, kf, vf, df = (rows[:FAR].astype(f32) for rows in (q, k, v, da))
     for h in range(H):
@@ -225,7 +224,6 @@
         remote(k_ref.at[near], k1, s_pair.at[0], r_pair.at[0], mate),
         remote(v_ref.at[near], v1, s_pair.at[1], r_pair.at[1], mate),
         remote(kt_ref.at[:, near], k1t, s_pair.at[2], r_pair.at[2], mate),
-        remote(vt_ref.at[:, near], v1t, s_pair.at[3], r_pair.at[3], mate),
     ]
     for copy in pair_copies:
         copy.start()
@@ -238,40 +236,41 @@
         mask0[:, 128 * c : 128 * c + 128] = jnp.where(open0, jnp.inf, 0.0).astype(bf16)
     row = iota((PAIR, 2 * PAIR), 0)
     mask1[...] = jnp.where(mate * T + place_of(row) < valid, jnp.inf, 0.0).astype(bf16)
-    dk[...] = jnp.zeros_like(dk)
-    dv[...] = jnp.zeros_like(dv)
-    dk1[...] = jnp.zeros_like(dk1)
-    dv1[...] = jnp.zeros_like(dv1)
 
     def place(g, hh):
         base, width, off = window(hh)
-        lanes = pl.ds(pl.multiple_of(g * 384 + base, 128), width)
-        rows = pl.ds(pl.multiple_of(g * 384 + W * hh, 16), W)
-        return lanes, rows, width, off
+        return pl.ds(g * 384 + base, width), pl.ds(g * 384 + W * hh, W), width, off
 
     def eight(g):
         return pl.ds(pl.multiple_of(g * PER, PER), PER)
 
-    def forward0(g):
-        totals = []
-        for hh in range(PER):
-            lanes, rows, width, off = place(g, hh)
-            ask = pad_rows(qt_ref[rows, :], off, width)
-            expo = jnp.exp2(dot(k_ref[:, lanes], ask)).astype(bf16)
-            expo = jnp.minimum(expo, mask0[...])
+    def scores(h):
+        lanes, rows, width, off = place(h // PER, h % PER)
+        return (
+            dot(k_ref[:, lanes], pad_rows(qt_ref[rows, :], off, width)),
+            dot(v_ref[:, lanes], pad_rows(dat_ref[rows, :], off, width)),
+        )
+
+    def column_sums(expo, dprob):
+        expo = expo.astype(f32)
+        return jnp.sum(expo, 0, keepdims=True), jnp.sum(expo * dprob, 0, keepdims=True)
+
+    def forward0(heads):
+        score, dprob = scores(heads[0])
+        for h in heads:
+            ahead = scores(h + 1) if h + 1 in heads else (None, None)
+            expo = jnp.minimum(jnp.exp2(score).astype(bf16), mask0[...])
             corner = expo[:PAIR, :PAIR]
             upper = jnp.concatenate([corner + corner, expo[:PAIR, PAIR:]], 1)
             expo = jnp.concatenate([upper, expo[PAIR:]], 0)
-            e0[g * PER + hh] = expo
-            value = jnp.concatenate([vt_ref[rows, :], jnp.ones((16, T), bf16)], 0)
-            mixed = dot(value, expo)
-            totals.append(mixed[W : W + 1])
-            mix[rows, :] = mixed[:W]
-        tot[eight(g), :] = jnp.concatenate(totals, 0)
+            e0[h] = expo
+            p0[h] = dprob.astype(bf16)
+            tot[h : h + 1, :], rsum[h : h + 1, :] = column_sums(expo, dprob)
+            score, dprob = ahead
 
     def pair_place(g, p):
         base, width, off = pair_window(p)
-        lanes = pl.ds(pl.multiple_of(g * 384 + base, 128), width)
+        lanes = pl.ds(g * 384 + base, width)
         low = pl.ds(pl.multiple_of(g * 384 + 2 * W * p, 16), W)
         high = pl.ds(pl.multiple_of(g * 384 + 2 * W * p + W, 16), W)
         both = pl.ds(pl.multiple_of(g * 384 + 2 * W * p, 16), 2 * W)
@@ -288,23 +287,22 @@
         return jnp.concatenate([rows * lane_mask(width, off), rows * lane_mask(width, off + W)], 0)
 
     def forward1(g):
-        totals = []
+        totals, sums = [], []
         for p in range(PER // 2):
             lanes, low, high, both, width, off = pair_place(g, p)
             ask = side_by_side(qt_ref[low, near], qt_ref[high, near], off, width)
-            expo = jnp.exp2(dot(k1[:, lanes], ask)).astype(bf16)
-            expo = jnp.minimum(expo, mask1[...])
+            given = side_by_side(dat_ref[low, near], dat_ref[high, near], off, width)
+            expo = jnp.minimum(jnp.exp2(dot(k1[:, lanes], ask)).astype(bf16), mask1[...])
+            dprob = dot(v1[:, lanes], given)
             e1[g * (PER // 2) + p] = expo
-            value = jnp.concatenate([v1t[both, :], jnp.ones((16, PAIR), bf16)], 0)
-            mixed = dot(value, expo)
-            mix[low, near] += mixed[:W, :PAIR]
-            mix[high, near] += mixed[W : 2 * W, PAIR:]
-            totals.append(mixed[2 * W : 2 * W + 1, :PAIR])
-            totals.append(mixed[2 * W : 2 * W + 1, PAIR:])
+            p1[g * (PER // 2) + p] = dprob.astype(bf16)
+            here, mixed = column_sums(expo, dprob)
+            totals += [here[:, :PAIR], here[:, PAIR:]]
+            sums += [mixed[:, :PAIR], mixed[:, PAIR:]]
         tot[eight(g), near] += jnp.concatenate(totals, 0)
-
-    for g in range(1):
-        forward0(g)
+        rsum[eight(g), near] += jnp.concatenate(sums, 0)
+
+    forward0(range(0, 10))
 
     drain(same, r_kv)
     drain(other, r_qd)
@@ -328,74 +326,94 @@
         jnp.where(lane >= 64, qda[...].astype(f32) * far_mixed, 0.0), 1, keepdims=True
     )
     far_t = far_mixed[:, 0:1]
-    send2[...] = jnp.where(lane == chip, far_t, 0.0) + jnp.where(lane == 64 + chip, far_r, 0.0)
+    far_parts = halves(far_t) + halves(far_r)
+    packed = jnp.zeros((256, 128), f32)
+    for i in range(4):
+        packed = packed + jnp.where(lane == 16 * i + chip, far_parts[i].astype(f32), 0.0)
+    send2[...] = packed.astype(bf16)
 
     for j in range(1, CHIPS):
         there = around(j)
         remote(send2.at[slot(there)], recv2.at[slot(chip)], s_2, r_2, there * 2 + core).start()
     pltpu.make_async_copy(send2.at[slot(chip)], recv2.at[slot(chip)], r_2).start()
 
-    forward0(1)
+    forward0(range(10, 16))
     for copy in pair_copies:
         copy.wait()
     for g in range(GROUPS):
         forward1(g)
 
     drain(recv2, r_2)
-    gathered = recv2[pl.ds(0, FAR)]
+    gathered = recv2[pl.ds(0, FAR)].astype(f32)
     for c in range(1, CHIPS):
-        gathered = gathered + recv2[pl.ds(c * FAR, FAR)]
+        gathered = gathered + recv2[pl.ds(c * FAR, FAR)].astype(f32)
     turned = jnp.concatenate([gathered, jnp.zeros((PAIR - FAR, 128), f32)], 0).T
-    tot[:, near] += turned[:H]
+    tot[:, near] += turned[:16] + turned[16:32]
     inverse = 1.0 / tot[...]
     tot[...] = inverse
-    far_sums = jnp.concatenate([turned[64 : 64 + H], jnp.zeros((H, T - PAIR), f32)], 1)
-    dlt[...] = far_sums * inverse * inverse
-    for h in range(H):
-        rows = pl.ds(W * h, W)
-        this = tot[h : h + 1, :]
-        scaled = (dat_ref[rows, :].astype(f32) * this).astype(bf16)
-        dapt[rows, :] = scaled
-        own = jnp.sum(scaled.astype(f32) * mix[rows, :], 0, keepdims=True)
-        dlt[h : h + 1, :] += own * this
-    filler = jnp.zeros((64 - H, 128), f32)
-    send3[...] = jnp.concatenate([tot[:, near], filler, dlt[:, near], filler], 0).T[:FAR]
+    rsum[:, near] += turned[32:48] + turned[48:64]
+    dlt[...] = rsum[...] * inverse * inverse
+    scale_parts = [part.astype(f32) for part in halves(tot[:, near]) + halves(dlt[:, near])]
+    scale_parts.append(jnp.zeros((64, 128), f32))
+    send3[...] = jnp.concatenate(scale_parts, 0).T[:FAR].astype(bf16)
 
     for j in range(1, CHIPS):
         there = around(j)
         remote(send3, recv3.at[slot(chip)], s_3, r_3, there * 2 + core).start()
     pltpu.make_async_copy(send3, recv3.at[slot(chip)], r_3).start()
-    dap[...] = dapt[...].T
-
-    def backward0(g):
-        deltas = dlt[eight(g), :]
-        for hh in range(PER):
-            lanes, rows, width, off = place(g, hh)
-            expo = e0[g * PER + hh]
-            dprob = dot(v_ref[:, lanes], pad_rows(dapt[rows, :], off, width))
-            dscore = expo * (dprob - deltas[hh : hh + 1]).astype(bf16)
-            e0[g * PER + hh] = dscore
+    scaled = []
+    for h in range(H):
+        rows = pl.ds(W * h, W)
+        scaled.append((dat_ref[rows, :].astype(f32) * tot[h : h + 1, :]).astype(bf16))
+    dap[...] = jnp.concatenate(scaled, 0).T
+
+    def gather_in(ref, lanes, width, value, fresh):
+        if width == 128:
+            if fresh:
+                ref[:, lanes] = value
+            else:
+                ref[:, lanes] += value
+        else:
+            ref[:, pl.ds(lanes.start, 128)] += value[:, :128]
+            ref[:, pl.ds(lanes.start + 128, 128)] = value[:, 128:]
+
+    def dscores(h):
+        dprob = p0[h].astype(f32) * tot[h : h + 1, :] - dlt[h : h + 1, :]
+        return e0[h] * dprob.astype(bf16)
+
+    def backward0(heads):
+        dscore = dscores(heads[0])
+        for h in heads:
+            lanes, rows, width, off = place(h // PER, h % PER)
+            value = dot(e0[h], dap[:, lanes] * lane_mask(width, off))
+            gather_in(dv, lanes, width, value, h % PER == 0)
+            ahead = dscores(h + 1) if h + 1 in heads else None
+            p0[h] = dscore
             dqt[rows, :] = dot(kt_ref[rows, :], dscore)
-            dv[:, lanes] += dot(expo, dap[:, lanes] * lane_mask(width, off))
+            dscore = ahead
 
     def backward1(g):
-        deltas = dlt[eight(g), near]
         for p in range(PER // 2):
             lanes, low, high, both, width, off = pair_place(g, p)
             expo = e1[g * (PER // 2) + p]
-            dprob = dot(v1[:, lanes], side_by_side(dapt[low, near], dapt[high, near], off, width))
-            delta = jnp.concatenate([deltas[2 * p : 2 * p + 1], deltas[2 * p + 1 : 2 * p + 2]], 1)
-            dscore = expo * (dprob - delta).astype(bf16)
+            a, b = g * PER + 2 * p, g * PER + 2 * p + 1
+            scale = jnp.concatenate([tot[a : a + 1, near], tot[b : b + 1, near]], 1)
+            delta = jnp.concatenate([dlt[a : a + 1, near], dlt[b : b + 1, near]], 1)
+            dprob = p1[g * (PER // 2) + p].astype(f32) * scale - delta
+            dscore = expo * dprob.astype(bf16)
             dq = dot(k1t[both, :], dscore)
             dq1t[low, :] = dq[:W, :PAIR]
             dq1t[high, :] = dq[W:, PAIR:]
-            dv1[:, lanes] += dot(expo, stacked(dap[near, lanes], off, width))
-            dk1[:, lanes] += dot(dscore, stacked(q_ref[near, lanes], off, width))
+            value = dot(expo, stacked(dap[near, lanes], off, width))
+            gather_in(dv1, lanes, width, value, p == 0)
+            value = dot(dscore, stacked(q_ref[near, lanes], off, width))
+            gather_in(dk1, lanes, width, value, p == 0)
 
     def keys0(g):
         for hh in range(PER):
             lanes, rows, width, off = place(g, hh)
-            dk[:, lanes] += dot(e0[g * PER + hh], q_ref[:, lanes] * lane_mask(width, off))
+            value = dot(p0[g * PER + hh], q_ref[:, lanes] * lane_mask(width, off))
+            gather_in(dk, lanes, width, value, hh == 0)
 
     for g in range(GROUPS):
         backward1(g)
@@ -403,12 +421,13 @@
     gsend[1] = dv1[...].astype(bf16)
     grad_copy = remote(gsend, gback, s_g, r_g, mate)
     grad_copy.start()
-    backward0(0)
+    backward0(range(0, 4))
 
     drain(recv3, r_3)
-    scales = recv3[...]
-    far_inv = jnp.sum(jnp.where(lane == chip, scales, 0.0), 1, keepdims=True)
-    far_del = jnp.sum(jnp.where(lane == 64 + chip, scales, 0.0), 1, keepdims=True)
+    scales = recv3[...].astype(f32)
+    for_head = (lane & 15) == chip
+    far_inv = jnp.sum(jnp.where(for_head & (lane < 32), scales, 0.0), 1, keepdims=True)
+    far_del = jnp.sum(jnp.where(for_head & (lane >= 32), scales, 0.0), 1, keepdims=True)
     far_grads = jnp.where(lane >= 64, qda[...].astype(f32) * far_inv, 0.0).astype(bf16)
     far_back = fe[...].astype(f32)
     far_ds = far_back * (dot_nt(far_grads, kv[...] * high) - far_del)
@@ -429,7 +448,7 @@
         ).start()
     pltpu.make_async_copy(bsame.at[slot(chip)], rsame.at[slot(chip)], r_4).start()
 
-    backward0(1)
+    backward0(range(4, 16))
 
     grad_copy.wait()
     drain(rsame, r_4)
@@ -444,12 +463,10 @@
     few = pl.ds(0, FAR)
     dv[near] += gback[1].astype(f32)
     dv[few] += jnp.concatenate(values_back, 1)
-    dk[near] = gback[0].astype(f32)
-    dk[few] += jnp.concatenate(keys_back, 1)
     dqt[:, near] += dq1t[...]
-    gq = dqt[...].T
-    gq = jnp.concatenate([gq[:FAR] + jnp.concatenate(asks_back, 1), gq[FAR:]], 0)
-    gq = (gq * SHARP).astype(bf16)
+    gq = (dqt[...] * SHARP).astype(bf16).T
+    first_rows = dqt[:, near].T[:FAR] + jnp.concatenate(asks_back, 1)
+    gq = jnp.concatenate([(first_rows * SHARP).astype(bf16), gq[FAR:]], 0)
     gv = dv[...].astype(bf16)
     back = dot_nt(gq, uq) + dot_nt(gv, uv)
     back_both = jnp.concatenate(halves(back), 1)
@@ -474,7 +491,7 @@
 
         @pl.when(there < SLICES)
         def _():
-            remote_to(part.at[there], one.at[mine], s_6, r_6, near_peer(j)).start()
+            remote_to(part.at[there], one.at[mine], s_6, r_6, plane_peer(j)).start()
 
         return carry
 
@@ -493,9 +510,11 @@
         total[0] = jnp.sum(one[...].astype(f32), 0).astype(bf16)
 
         for j in range(1, 16):
-            remote_to(total.at[0], two.at[plane], s_7, r_7, across_peer(j)).start()
-        pltpu.make_async_copy(total.at[0], two.at[plane], r_7).start()
-
+            remote_to(total.at[0], two.at[column], s_7, r_7, column_peer(j)).start()
+        pltpu.make_async_copy(total.at[0], two.at[column], r_7).start()
+
+    dk[near] += gback[0].astype(f32)
+    dk[few] += jnp.concatenate(keys_back, 1)
     gk = (dk[...] * LN2).astype(bf16)
     grad = (
         dot_nt(gq, wq_ref[...])
@@ -512,16 +531,25 @@
         total[1] = both_sum.astype(bf16)
 
         for j in range(1, 16):
-            remote_to(total.at[1], done.at[mine], s_8, r_8, near_peer(j)).start()
+            remote_to(total.at[1], done.at[mine], s_8, r_8, plane_peer(j)).start()
         pltpu.make_async_copy(total.at[1], done.at[mine], r_8).start()
 
     xhat = xhat_s[...]
     out = scale_s[:, 0:1] * (
         s - jnp.mean(s, -1, keepdims=True) - xhat * jnp.mean(s * xhat, -1, keepdims=True)
     )
-    out_ref[...] = out.astype(bf16)
+    unorder = jnp.where(place_of(iota((1, T), 1)) == iota((T, T), 0), 1.0, 0.0).astype(bf16)
+    out_s[0] = dot(unorder, out.astype(bf16)).astype(bf16)
+    leave = pltpu.make_async_copy(out_s, out_ref, s_out)
+    leave.start()
     drain(done, r_8)
-
+    for p in range(2):
+        for c in range(6):
+            tile = done[p * 6 + c].astype(f32)
+            merged_ref[2 * p, :, 128 * c : 128 * c + 128] = tile[:R]
+            merged_ref[2 * p + 1, :, 128 * c : 128 * c + 128] = tile[R:]
+
+    leave.wait()
     drain(same.at[pl.ds(0, (CHIPS - 1) * FAR)], s_kv)
     drain(other, s_qd)
     drain(recv2.at[pl.ds(0, (CHIPS - 1) * FAR)], s_2)
@@ -540,14 +568,15 @@
         drain(one.at[pl.ds(0, SLICES)], s_6)
 
 
-def place_kernel(y_ref, done_ref, out_ref, merged_ref):
-    unorder = jnp.where(place_of(iota((1, T), 1)) == iota((T, T), 0), 1.0, 0.0).astype(bf16)
-    out_ref[0] = dot(unorder, y_ref[...]).astype(bf16)
-    for p in range(2):
-        for c in range(6):
-            tile = done_ref[p * 6 + c].astype(f32)
-            merged_ref[2 * p, :, 128 * c : 128 * c + 128] = tile[:R]
-            merged_ref[2 * p + 1, :, 128 * c : 128 * c + 128] = tile[R:]
+def hand_on_kernel(out_in, merged_in, out_ref, merged_ref, sems):
+    copies = [
+        pltpu.make_async_copy(out_in, out_ref, sems.at[0]),
+        pltpu.make_async_copy(merged_in, merged_ref, sems.at[1]),
+    ]
+    for copy in copies:
+        copy.start()
+    for copy in copies:
+        copy.wait()
 
 
 def shape(*dims, kind=bf16):
@@ -568,36 +597,37 @@
 ):
     buf = pltpu.VMEM
     sem = pltpu.SemaphoreType.DMA
-    y, done = pl.pallas_call(
+    out, merged = pl.pallas_call(
         layer_kernel,
-        out_shape=[shape(T, D), shape(SLICES, 16, 128)],
+        out_shape=[shape(1, T, D), shape(4, R, D, kind=f32)],
         in_specs=[pl.BlockSpec(memory_space=pltpu.SMEM), whole(), far(), whole()] + [far()] * 4
         + [whole()] * 4,
-        out_specs=[whole()] * 2,
+        out_specs=[far(), whole()],
         scratch_shapes=[
             buf((1, T, D), bf16), buf((D, D), bf16), buf((D, D), bf16), buf((D, D), bf16),
-            buf((D, D), bf16), sem((5,)),
+            buf((D, D), bf16), sem((5,)), buf((1, T, D), bf16), sem,
             buf((T, D), f32), buf((T, 128), f32), buf((T, D), bf16), buf((2 * R, T), f32),
             buf((T, D), bf16), buf((T, D), bf16), buf((T, D), bf16),
-            buf((D, T), bf16), buf((D, T), bf16), buf((D, T), bf16), buf((D, T), bf16),
+            buf((D, T), bf16), buf((D, T), bf16), buf((D, T), bf16),
             buf((H, FAR, 256), bf16),
-            buf((H, T, T), bf16), buf((H // 2, PAIR, 256), bf16),
+            buf((H, T, T), bf16), buf((H, T, T), bf16),
+            buf((H // 2, PAIR, 256), bf16), buf((H // 2, PAIR, 256), bf16),
             buf((T, T), bf16), buf((PAIR, 256), bf16),
-            buf((H, T), f32), buf((D, T), f32), buf((H, T), f32),
-            buf((D, T), bf16), buf((T, D), bf16), buf((D, T), f32), buf((D, PAIR), f32),
+            buf((H, T), f32), buf((H, T), f32), buf((H, T), f32),
+            buf((T, D), bf16), buf((D, T), f32), buf((D, PAIR), f32),
             buf((T, D), f32), buf((T, D), f32),
-            buf((PAIR, D), bf16), buf((PAIR, D), bf16), buf((D, PAIR), bf16), buf((D, PAIR), bf16),
+            buf((PAIR, D), bf16), buf((PAIR, D), bf16), buf((D, PAIR), bf16),
             buf((PAIR, D), f32), buf((PAIR, D), f32),
             buf((2, PAIR, D), bf16), buf((2, PAIR, D), bf16),
             buf((256, 256), bf16), buf((256, 128), bf16),
             buf((T, 128), bf16), buf((256, 128), bf16), buf((256, T), bf16),
-            buf((256, 128), f32), buf((256, 128), f32),
-            buf((FAR, 128), f32), buf((256, 128), f32),
+            buf((256, 128), bf16), buf((256, 128), bf16),
+            buf((FAR, 128), bf16), buf((256, 128), bf16),
             buf((256, 256), bf16), buf((256, 128), bf16),
             buf((256, 256), bf16), buf((256, 128), bf16),
             buf((SLICES, 16, 128), bf16), buf((16, 16, 128), bf16), buf((2, 16, 128), bf16),
-            buf((16, 16, 128), bf16),
-            sem, sem, sem, sem, sem((4,)), sem((4,)), sem, sem, sem, sem, sem, sem, sem, sem,
+            buf((16, 16, 128), bf16), buf((SLICES, 16, 128), bf16),
+            sem, sem, sem, sem, sem((3,)), sem((3,)), sem, sem, sem, sem, sem, sem, sem, sem,
             sem, sem, sem, sem, sem, sem, sem, sem,
         ],
         compiler_params=pltpu.CompilerParams(
@@ -609,12 +639,13 @@
         query_down_factor.T, query_up_factor, value_down_factor.T, value_up_factor,
     )
     return pl.pallas_call(
-        place_kernel,
+        hand_on_kernel,
         out_shape=[shape(1, T, D), shape(4, R, D, kind=f32)],
         in_specs=[whole()] * 2,
-        out_specs=[whole()] * 2,
-        name="place",
-    )(y, done)
+        out_specs=[far()] * 2,
+        scratch_shapes=[sem((2,))],
+        name="hand_on",
+    )(out, merged)
 
 
 def solution(mesh):

time: 66.2 us -> 61.9 us (0.935)
  Pallas kernels: 64.7 us -> 60.3 us
    pallas_call x2, Pallas kernels: 64.7 us -> 60.3 us  [the longest x1 58.2 us: per_device(): pl.pallas_call(layer_kernel, out_shape=[shape(1, T, D), shape(4, R, D, ki...]
where the time goes in v3:
time: 61.9 us; the launch traced here: 61.8 us
  Pallas kernels  60.3 us (97%)
  between operations  1.47 us (2%)
    pallas_call x1, Pallas kernels, per_device(): pl.pallas_call(layer_kernel, out_shape=[shape(1, T, D), shape(4, R, D, ki...  58.2 us
    pallas_call x1, Pallas kernels, per_device(): pl.pallas_call(hand_on_kernel, out_shape=[shape(1, T, D), shape(4, R, D,...  2.05 us

profile of v3, /device:TPU:1, one launch (start us, length us, event | category | flops | bytes accessed | tf_op | source)
XLA Modules:
  0.0 61.8 jit_solution(11173464845018673818)
XLA Ops:
  1.3 58.2 %layer.1 = (bf16[1,512,768]{2,1,0:T(8,128)(2,1)}, f32[4,8,768]{2,1,0:T(8,128)}) custom-call(s32[1]{0:T(128)S(6)} %copy.14.valid_ref, bf16[1,512,768]{2,1,0:T(8,128)(2,1)} %tiles_ref.1, bf16[1,512,768]{2,1,0:T(8,128)(2,1)} %cot_hbm.1, bf16[768]{0:T(1024)(128)(2,1)} %gain_ref.1, bf16[768,768]{1,0:T(8,128)(2,1)} %wq_hbm.1, bf16[768,768]{1,0:T(8,128)(2,1)} %wk_hbm.1, ...), custom_call_target="tpu_custom_call" | custom-call | tf_op jit(solution)/shard_map/layer/pallas_call | solution.py:600
  59.5 2.1 %hand_on.1 = (bf16[1,512,768]{2,1,0:T(8,128)(2,1)}, f32[4,8,768]{2,1,0:T(8,128)}) custom-call(bf16[1,512,768]{2,1,0:T(8,128)(2,1)} %get-tuple-element.4.out_in, f32[4,8,768]{2,1,0:T(8,128)} %get-tuple-element.5.merged_in), custom_call_target="tpu_custom_call" | custom-call | tf_op jit(solution)/shard_map/hand_on/pallas_call | solution.py:641

commit v4 on v3

--- a/solution.py
+++ b/solution.py
@@ -244,28 +244,54 @@
     def eight(g):
         return pl.ds(pl.multiple_of(g * PER, PER), PER)
 
-    def scores(h):
-        lanes, rows, width, off = place(h // PER, h % PER)
-        return (
-            dot(k_ref[:, lanes], pad_rows(qt_ref[rows, :], off, width)),
-            dot(v_ref[:, lanes], pad_rows(dat_ref[rows, :], off, width)),
-        )
-
     def column_sums(expo, dprob):
         expo = expo.astype(f32)
         return jnp.sum(expo, 0, keepdims=True), jnp.sum(expo * dprob, 0, keepdims=True)
 
     def forward0(heads):
-        score, dprob = scores(heads[0])
-        for h in heads:
-            ahead = scores(h + 1) if h + 1 in heads else (None, None)
-            expo = jnp.minimum(jnp.exp2(score).astype(bf16), mask0[...])
-            corner = expo[:PAIR, :PAIR]
-            upper = jnp.concatenate([corner + corner, expo[:PAIR, PAIR:]], 1)
-            expo = jnp.concatenate([upper, expo[PAIR:]], 0)
-            e0[h] = expo
-            p0[h] = dprob.astype(bf16)
-            tot[h : h + 1, :], rsum[h : h + 1, :] = column_sums(expo, dprob)
+        def operands(h, c):
+            lanes, rows, width, off = place(h // PER, h % PER)
+            cols = pl.ds(256 * c, 256)
+            return (
+                lanes, pad_rows(qt_ref[rows, cols], off, width),
+                pad_rows(dat_ref[rows, cols], off, width),
+            )
+
+        def products(given, b):
+            lanes, ask, grad = given
+            block = pl.ds(128 * b, 128)
+            return dot(k_ref[block, lanes], ask), dot(v_ref[block, lanes], grad)
+
+        def fold(value):
+            return jnp.sum(value.reshape(16, 8, 256), 0)
+
+        steps = [(h, c, b) for h in heads for c in range(2) for b in range(4)]
+        given = operands(heads[0], 0)
+        score, dprob = products(given, 0)
+        total = mixed = None
+        for n, (h, c, b) in enumerate(steps):
+            ahead = (None, None)
+            if n + 1 < len(steps):
+                after = steps[n + 1]
+                if after[2] == 0:
+                    given = operands(after[0], after[1])
+                ahead = products(given, after[2])
+            block = pl.ds(128 * b, 128)
+            cols = pl.ds(256 * c, 256)
+            expo = jnp.minimum(jnp.exp2(score).astype(bf16), mask0[block, cols])
+            if c == 0 and b == 0:
+                corner = expo[:, :PAIR]
+                expo = jnp.concatenate([corner + corner, expo[:, PAIR:]], 1)
+            e0[h, block, cols] = expo
+            p0[h, block, cols] = dprob.astype(bf16)
+            wide = expo.astype(f32)
+            if b == 0:
+                total, mixed = fold(wide), fold(wide * dprob)
+            else:
+                total, mixed = total + fold(wide), mixed + fold(wide * dprob)
+            if b == 3:
+                tot[h : h + 1, cols] = jnp.sum(total, 0, keepdims=True)
+                rsum[h : h + 1, cols] = jnp.sum(mixed, 0, keepdims=True)
             score, dprob = ahead
 
     def pair_place(g, p):

time: 61.9 us -> 61.5 us (level)
  no operation moved by 1% of the time
where the time goes in v4:
time: 61.5 us; the launch traced here: 61.3 us
  Pallas kernels  59.9 us (97%)
  between operations  1.47 us (2%)
    pallas_call x1, Pallas kernels, per_device(): pl.pallas_call(layer_kernel, out_shape=[shape(1, T, D), shape(4, R, D, ki...  57.8 us
    pallas_call x1, Pallas kernels, per_device(): pl.pallas_call(hand_on_kernel, out_shape=[shape(1, T, D), shape(4, R, D,...  2.05 us

profile of v4, /device:TPU:1, one launch (start us, length us, event | category | flops | bytes accessed | tf_op | source)
XLA Modules:
  0.0 61.3 jit_solution(14771905267528031115)
XLA Ops:
  1.3 57.8 %layer.1 = (bf16[1,512,768]{2,1,0:T(8,128)(2,1)}, f32[4,8,768]{2,1,0:T(8,128)}) custom-call(s32[1]{0:T(128)S(6)} %copy.14.valid_ref, bf16[1,512,768]{2,1,0:T(8,128)(2,1)} %tiles_ref.1, bf16[1,512,768]{2,1,0:T(8,128)(2,1)} %cot_hbm.1, bf16[768]{0:T(1024)(128)(2,1)} %gain_ref.1, bf16[768,768]{1,0:T(8,128)(2,1)} %wq_hbm.1, bf16[768,768]{1,0:T(8,128)(2,1)} %wk_hbm.1, ...), custom_call_target="tpu_custom_call" | custom-call | tf_op jit(solution)/shard_map/layer/pallas_call | solution.py:626
  59.1 2.1 %hand_on.1 = (bf16[1,512,768]{2,1,0:T(8,128)(2,1)}, f32[4,8,768]{2,1,0:T(8,128)}) custom-call(bf16[1,512,768]{2,1,0:T(8,128)(2,1)} %get-tuple-element.4.out_in, f32[4,8,768]{2,1,0:T(8,128)} %get-tuple-element.5.merged_in), custom_call_target="tpu_custom_call" | custom-call | tf_op jit(solution)/shard_map/hand_on/pallas_call | solution.py:667

commit v5 on v4

--- a/solution.py
+++ b/solution.py
@@ -46,9 +46,9 @@
     return (row & 15) * 32 + ((row >> 4) & 7) * 4 + (row >> 7)
 
 
-def order_matrix():
-    place = place_of(iota((T, 128), 0))
-    lane = iota((T, 128), 1)
+def order_matrix(first, count):
+    place = place_of(first + iota((count, 128), 0))
+    lane = iota((count, 128), 1)
     parts = [jnp.where(place == lane + 128 * c, 1.0, 0.0) for c in range(4)]
     return jnp.concatenate(parts, 1).astype(bf16)
 
@@ -166,36 +166,43 @@
     for load in loads:
         load.start()
 
-    order = order_matrix()
-    x = dot(order, tiles_ref[0])
-    loads[0].wait()
-    loads[1].wait()
-    cot = dot(order, cot_ref[0]).astype(bf16)
-    da = dot_nt(cot, wo_ref[...]).astype(bf16)
-    dat_ref[...] = da.T
-    xhat, inverse_dev = normalize(x)
-    xhat_s[...] = xhat
-    scale_s[...] = jnp.broadcast_to(inverse_dev, (T, 128))
-    normed = (xhat * gain_ref[...].astype(f32)).astype(bf16)
-    normed_s[...] = normed
     down = down_rows(qd_ref, vd_ref)
     uq = up_padded(qu_ref, 0)
     uv = up_padded(vu_ref, R)
-    lift = dot_nt(normed, down)
-    both = jnp.concatenate(halves(lift), 1)
-    lift_s[...] = lift.T[: 2 * R]
-    loads[2].wait()
-    loads[3].wait()
-    loads[4].wait()
-    q = dot(normed, wq_ref[...]) + 2.0 * dot(both, jnp.concatenate([uq, uq], 0))
-    q = (q * (SHARP * LOG2E)).astype(bf16)
-    q_ref[...] = q
-    qt_ref[...] = q.T
-    k = dot(normed, wk_ref[...]).astype(bf16)
-    k_ref[...] = k
-    kt_ref[...] = k.T
-    v = (dot(normed, wv_ref[...]) + 2.0 * dot(both, jnp.concatenate([uv, uv], 0))).astype(bf16)
-    v_ref[...] = v
+
+    def project(first, count, arrive):
+        some = pl.ds(first, count)
+        order = order_matrix(first, count)
+        x = dot(order, tiles_ref[0])
+        arrive(0, 1)
+        cot = dot(order, cot_ref[0]).astype(bf16)
+        da = dot_nt(cot, wo_ref[...]).astype(bf16)
+        dat_ref[:, some] = da.T
+        xhat, inverse_dev = normalize(x)
+        xhat_s[some] = xhat
+        scale_s[some] = jnp.broadcast_to(inverse_dev, (count, 128))
+        normed = (xhat * gain_ref[...].astype(f32)).astype(bf16)
+        normed_s[some] = normed
+        lift = dot_nt(normed, down)
+        both = jnp.concatenate(halves(lift), 1)
+        lift_s[:, some] = lift.T[: 2 * R]
+        arrive(2, 3, 4)
+        q = dot(normed, wq_ref[...]) + 2.0 * dot(both, jnp.concatenate([uq, uq], 0))
+        q = (q * (SHARP * LOG2E)).astype(bf16)
+        q_ref[some] = q
+        qt_ref[:, some] = q.T
+        k = dot(normed, wk_ref[...]).astype(bf16)
+        k_ref[some] = k
+        kt_ref[:, some] = k.T
+        v = (dot(normed, wv_ref[...]) + 2.0 * dot(both, jnp.concatenate([uv, uv], 0))).astype(bf16)
+        v_ref[some] = v
+        return q, k, v, da
+
+    def arrive(*which):
+        for i in which:
+            loads[i].wait()
+
+    q, k, v, da = project(0, PAIR, arrive)
     gap = jnp.zeros((FAR, 64 - W), f32)
     qf, kf, vf, df = (rows[:FAR].astype(f32) for rows in (q, k, v, da))
     for h in range(H):
@@ -227,6 +234,8 @@
     ]
     for copy in pair_copies:
         copy.start()
+
+    project(PAIR, T - PAIR, lambda *which: None)
 
     row = iota((T, 128), 0)
     col = iota((T, 128), 1)
@@ -328,7 +337,7 @@
         tot[eight(g), near] += jnp.concatenate(totals, 0)
         rsum[eight(g), near] += jnp.concatenate(sums, 0)
 
-    forward0(range(0, 10))
+    forward0(range(0, 6))
 
     drain(same, r_kv)
     drain(other, r_qd)
@@ -363,7 +372,7 @@
         remote(send2.at[slot(there)], recv2.at[slot(chip)], s_2, r_2, there * 2 + core).start()
     pltpu.make_async_copy(send2.at[slot(chip)], recv2.at[slot(chip)], r_2).start()
 
-    forward0(range(10, 16))
+    forward0(range(6, 16))
     for copy in pair_copies:
         copy.wait()
     for g in range(GROUPS):

time: 61.5 us -> 59 us (0.959)
  Pallas kernels: 59.9 us -> 57.4 us
    pallas_call x1, Pallas kernels: 57.8 us -> 55.3 us  [per_device(): pl.pallas_call(layer_kernel, out_shape=[shape(1, T, D), shape(4, R, D, ki...]
where the time goes in v5:
time: 59 us; the launch traced here: 58.9 us
  Pallas kernels  57.4 us (97%)
  between operations  1.47 us (2%)
    pallas_call x1, Pallas kernels, per_device(): pl.pallas_call(layer_kernel, out_shape=[shape(1, T, D), shape(4, R, D, ki...  55.3 us
    pallas_call x1, Pallas kernels, per_device(): pl.pallas_call(hand_on_kernel, out_shape=[shape(1, T, D), shape(4, R, D,...  2.05 us

profile of v5, /device:TPU:1, one launch (start us, length us, event | category | flops | bytes accessed | tf_op | source)
XLA Modules:
  0.0 58.9 jit_solution(12133414284200024401)
XLA Ops:
  1.3 55.3 %layer.1 = (bf16[1,512,768]{2,1,0:T(8,128)(2,1)}, f32[4,8,768]{2,1,0:T(8,128)}) custom-call(s32[1]{0:T(128)S(6)} %copy.14.valid_ref, bf16[1,512,768]{2,1,0:T(8,128)(2,1)} %tiles_ref.1, bf16[1,512,768]{2,1,0:T(8,128)(2,1)} %cot_hbm.1, bf16[768]{0:T(1024)(128)(2,1)} %gain_ref.1, bf16[768,768]{1,0:T(8,128)(2,1)} %wq_hbm.1, bf16[768,768]{1,0:T(8,128)(2,1)} %wk_hbm.1, ...), custom_call_target="tpu_custom_call" | custom-call | tf_op jit(solution)/shard_map/layer/pallas_call | solution.py:635
  56.6 2.1 %hand_on.1 = (bf16[1,512,768]{2,1,0:T(8,128)(2,1)}, f32[4,8,768]{2,1,0:T(8,128)}) custom-call(bf16[1,512,768]{2,1,0:T(8,128)(2,1)} %get-tuple-element.4.out_in, f32[4,8,768]{2,1,0:T(8,128)} %get-tuple-element.5.merged_in), custom_call_target="tpu_custom_call" | custom-call | tf_op jit(solution)/shard_map/hand_on/pallas_call | solution.py:676

commit v6 on v5

--- a/solution.py
+++ b/solution.py
@@ -378,16 +378,30 @@
     for g in range(GROUPS):
         forward1(g)
 
+    wide = pl.ds(PAIR, T - PAIR)
+
+    def settle(cols):
+        inverse = 1.0 / tot[:, cols]
+        tot[:, cols] = inverse
+        dlt[:, cols] = rsum[:, cols] * inverse * inverse
+
+    def scale_grads(cols):
+        scaled = []
+        for h in range(H):
+            part_t = dat_ref[pl.ds(W * h, W), cols].astype(f32)
+            scaled.append((part_t * tot[h : h + 1, cols]).astype(bf16))
+        dap[cols] = jnp.concatenate(scaled, 0).T
+
+    settle(wide)
+    scale_grads(wide)
     drain(recv2, r_2)
     gathered = recv2[pl.ds(0, FAR)].astype(f32)
     for c in range(1, CHIPS):
         gathered = gathered + recv2[pl.ds(c * FAR, FAR)].astype(f32)
     turned = jnp.concatenate([gathered, jnp.zeros((PAIR - FAR, 128), f32)], 0).T
     tot[:, near] += turned[:16] + turned[16:32]
-    inverse = 1.0 / tot[...]
-    tot[...] = inverse
     rsum[:, near] += turned[32:48] + turned[48:64]
-    dlt[...] = rsum[...] * inverse * inverse
+    settle(near)
     scale_parts = [part.astype(f32) for part in halves(tot[:, near]) + halves(dlt[:, near])]
     scale_parts.append(jnp.zeros((64, 128), f32))
     send3[...] = jnp.concatenate(scale_parts, 0).T[:FAR].astype(bf16)
@@ -396,11 +410,7 @@
         there = around(j)
         remote(send3, recv3.at[slot(chip)], s_3, r_3, there * 2 + core).start()
     pltpu.make_async_copy(send3, recv3.at[slot(chip)], r_3).start()
-    scaled = []
-    for h in range(H):
-        rows = pl.ds(W * h, W)
-        scaled.append((dat_ref[rows, :].astype(f32) * tot[h : h + 1, :]).astype(bf16))
-    dap[...] = jnp.concatenate(scaled, 0).T
+    scale_grads(near)
 
     def gather_in(ref, lanes, width, value, fresh):
         if width == 128:
@@ -486,6 +496,11 @@
     backward0(range(4, 16))
 
     grad_copy.wait()
+    dv[near] += gback[1].astype(f32)
+    dqt[:, near] += dq1t[...]
+    gq_rest = (dqt[...] * SHARP).astype(bf16).T
+    gq_first = dqt[:, near].T[:FAR]
+    lu, ll = halves(lift_s[...])
     drain(rsame, r_4)
     drain(rother, r_5)
     keys_back, values_back, asks_back = [], [], []
@@ -496,17 +511,13 @@
         values_back.append(here[:, 64 : 64 + W])
         asks_back.append(both_back[:, 128 : 128 + W])
     few = pl.ds(0, FAR)
-    dv[near] += gback[1].astype(f32)
     dv[few] += jnp.concatenate(values_back, 1)
-    dqt[:, near] += dq1t[...]
-    gq = (dqt[...] * SHARP).astype(bf16).T
-    first_rows = dqt[:, near].T[:FAR] + jnp.concatenate(asks_back, 1)
-    gq = jnp.concatenate([(first_rows * SHARP).astype(bf16), gq[FAR:]], 0)
+    first_rows = gq_first + jnp.concatenate(asks_back, 1)
+    gq = jnp.concatenate([(first_rows * SHARP).astype(bf16), gq_rest[FAR:]], 0)
     gv = dv[...].astype(bf16)
     back = dot_nt(gq, uq) + dot_nt(gv, uv)
     back_both = jnp.concatenate(halves(back), 1)
     bu, bl = halves(back.T[: 2 * R])
-    lu, ll = halves(lift_s[...])
     from_back = dot(jnp.concatenate([bu, bl], 0), normed_s[...])
     from_back = 2.0 * (from_back[:16] + from_back[16:])
     lifts = jnp.concatenate([lu, ll], 0)

time: 59 us -> 59 us (level)
  no operation moved by 1% of the time
where the time goes in v6:
time: 59 us; the launch traced here: 58.8 us
  Pallas kernels  57.4 us (97%)
  between operations  1.47 us (2%)
    pallas_call x1, Pallas kernels, per_device(): pl.pallas_call(layer_kernel, out_shape=[shape(1, T, D), shape(4, R, D, ki...  55.3 us
    pallas_call x1, Pallas kernels, per_device(): pl.pallas_call(hand_on_kernel, out_shape=[shape(1, T, D), shape(4, R, D,...  2.05 us

profile of v6, /device:TPU:1, one launch (start us, length us, event | category | flops | bytes accessed | tf_op | source)
XLA Modules:
  0.0 58.8 jit_solution(6307884300769415706)
XLA Ops:
  1.3 55.3 %layer.1 = (bf16[1,512,768]{2,1,0:T(8,128)(2,1)}, f32[4,8,768]{2,1,0:T(8,128)}) custom-call(s32[1]{0:T(128)S(6)} %copy.14.valid_ref, bf16[1,512,768]{2,1,0:T(8,128)(2,1)} %tiles_ref.1, bf16[1,512,768]{2,1,0:T(8,128)(2,1)} %cot_hbm.1, bf16[768]{0:T(1024)(128)(2,1)} %gain_ref.1, bf16[768,768]{1,0:T(8,128)(2,1)} %wq_hbm.1, bf16[768,768]{1,0:T(8,128)(2,1)} %wk_hbm.1, ...), custom_call_target="tpu_custom_call" | custom-call | tf_op jit(solution)/shard_map/layer/pallas_call | solution.py:646
  56.6 2.1 %hand_on.1 = (bf16[1,512,768]{2,1,0:T(8,128)(2,1)}, f32[4,8,768]{2,1,0:T(8,128)}) custom-call(bf16[1,512,768]{2,1,0:T(8,128)(2,1)} %get-tuple-element.4.out_in, f32[4,8,768]{2,1,0:T(8,128)} %get-tuple-element.5.merged_in), custom_call_target="tpu_custom_call" | custom-call | tf_op jit(solution)/shard_map/hand_on/pallas_call | solution.py:687
